TPU v7x, 32 devices: a whole 2x2x4 slice. The times are simulated.
32 devices in a mesh: ctx: 4 (over y, x), tile: 8 (over z, core).
Axes of the slice: x: 2, y: 2, z: 4, core: 2. Of those that a mesh axis runs over, the one named last changes fastest.
Arguments:
- syndrome_bits: int32 [8, 2, 32, 256], P(None, None, 'ctx', 'tile'), may hold values from 0 to 1
- region_assign: int32 [16, 128], P('ctx', 'tile'), may hold values from 0 to 127
- state_in: bfloat16 [32, 256, 512], P('ctx', 'tile'), may hold values from -3 to 3
- bit_to_candidate: float32 [2, 512], replicated, may hold values from -5 to 5
- bit_to_gate: float32 [2, 512], replicated, may hold values from -5 to 5
- conv_weight: bfloat16 [9, 512, 512], replicated, may hold values from -0.09375 to 0.09375
- gate_weight: bfloat16 [512, 512], replicated, may hold values from -0.25 to 0.25
- gate_bias: float32 [512], replicated, may hold values from -4 to 1
- pool_weight: bfloat16 [512, 1024], replicated, may hold values from -0.25 to 0.25
- region_embed: bfloat16 [512, 1024], P('ctx'), may hold values from -6 to 6
- attn_norm_gain: float32 [1024], replicated, may hold values from 0.1 to 1.9
- query_weight: bfloat16 [1024, 1024], replicated
- key_weight: bfloat16 [1024, 1024], replicated
- value_weight: bfloat16 [1024, 1024], replicated, may hold values from -0.1875 to 0.1875
- out_weight: bfloat16 [1024, 1024], replicated, may hold values from -0.1875 to 0.1875
- mlp_norm_gain: float32 [1024], replicated, may hold values from 0.1 to 1.9
- mlp_up: bfloat16 [1024, 2048], replicated, may hold values from -0.1875 to 0.1875
- mlp_down: bfloat16 [2048, 1024], replicated, may hold values from -0.125 to 0.125
- return_weight: bfloat16 [1024, 512], replicated, may hold values from -0.1875 to 0.1875
Outputs:
- state_out: bfloat16 [32, 256, 512], P('ctx', 'tile')
- context_out: bfloat16 [512, 1024], P('ctx')
All inputs are finite; a program needn't handle non-finite values.
Results may differ from a plain program's by a relative error of at most 0.02.
Values may be sent and summed in bfloat16 or wider, within the bound.
No kernel may reach another device: no remote copies, remote signals or barrier semaphores. Data moves between devices by JAX's collectives and lax.ppermute only.
A program may use at most 128 MiB of HBM per device.

v0:
```python
import functools
import math

import jax
import jax.numpy as jnp
from jax import lax
from jax.experimental import pallas as pl
from jax.experimental.pallas import tpu as pltpu
from jax.sharding import PartitionSpec as P

HEADS = 8
HDIM = 128
ROUNDS = 8
HALF = ROUNDS // 2
LANES = 128
F32 = jnp.float32
BF16 = jnp.bfloat16
MIB = 2**20

TILE = ("chip", "core")

REGION_LANE, LOW_LANE, ONE_LANE = 2 * ROUNDS, 32, 64


def shifted(value, axis, step):
    size = math.prod(lax.axis_size(name) for name in axis)
    pairs = [(i, i + step) for i in range(size) if 0 <= i + step < size]
    return lax.ppermute(value, axis, pairs)


def row_halo(top, bottom):
    return shifted(bottom, ("ctx",), 1), shifted(top, ("ctx",), -1)


def col_halo(cols, above, first, last, below):
    count, lanes = first.shape
    first, last = call(
        functools.partial(edges_kernel, cols),
        "edges",
        (above, first, last, below),
        [array(2 * count, lanes, BF16)] * 2,
        grant=8,
    )
    return shifted(last, TILE, 1), shifted(first, TILE, -1)


def matmul(left, right):
    return jnp.dot(left, right, preferred_element_type=F32)


def matmul_nt(left, right):
    return lax.dot_general(left, right, (((1,), (1,)), ((), ())), preferred_element_type=F32)


def two_parts(values):
    high = values.astype(BF16)
    return high, (values - high.astype(F32)).astype(BF16)


def select(member, values):
    high, low = two_parts(values)
    return matmul(member, high) + matmul(member, low)


def rms_norm(values, gain):
    return values * lax.rsqrt(jnp.mean(values * values, axis=-1, keepdims=True) + 1e-05) * gain


def iota(shape, dim):
    return lax.broadcasted_iota(jnp.int32, shape, dim)


def one_hot(condition):
    return jnp.where(condition, 1.0, 0.0).astype(BF16)


def call(kernel, name, operands, outs, scratch=(), in_hbm=(), scalars=(), grant=60, flops=0, moved=MIB):
    def spec(index):
        if index in in_hbm:
            return pl.BlockSpec(memory_space=pltpu.HBM)
        return pl.BlockSpec(memory_space=pltpu.SMEM if index in scalars else pltpu.VMEM)

    return pl.pallas_call(
        kernel,
        out_shape=outs,
        in_specs=[spec(index) for index in range(len(operands))],
        out_specs=[pl.BlockSpec(memory_space=pltpu.VMEM)] * len(outs),
        scratch_shapes=scratch,
        compiler_params=pltpu.CompilerParams(vmem_limit_bytes=grant * MIB),
        cost_estimate=pl.CostEstimate(flops=flops, bytes_accessed=moved, transcendentals=0),
        name=name,
    )(*operands)


def array(count, lanes, dtype):
    return jax.ShapeDtypeStruct((count, lanes), dtype)


def first_columns(part, cols, begin):
    values = part[...].astype(F32)
    return [values[at + begin : at + begin + HALF] for at in range(0, part.shape[0], cols)]


def edges_kernel(cols, above, own_first, own_last, below, first, last):
    for own, begin, out in ((own_first, 0, first), (own_last, cols - HALF, last)):
        parts = first_columns(above, cols, begin) + [own[...].astype(F32)] + first_columns(below, cols, begin)
        out[...] = jnp.concatenate(parts).astype(BF16)


def patch_outputs(half, lanes):
    return [array(half, lanes, BF16)] * 2 + [array(2 * HALF * HALF, lanes, BF16)] * 2


def write_patch(outs, rows):
    top, bottom, first, last = outs
    cols = rows[0].shape[0]
    for r, values in enumerate(rows):
        half = (top, bottom)[r // HALF]
        half[r % HALF * cols : (r % HALF + 1) * cols] = values.astype(BF16)
    first[...] = jnp.concatenate([values[:HALF] for values in rows]).astype(BF16)
    last[...] = jnp.concatenate([values[cols - HALF :] for values in rows]).astype(BF16)


def message_kernel(syndrome, region, state, *outs):
    planes, rows, cols = syndrome.shape
    bits = syndrome[...].reshape(planes * rows, cols).astype(F32).astype(BF16)
    column_bits = matmul_nt(one_hot(iota((cols, cols), 0) == iota((cols, cols), 1)), bits).astype(BF16)
    block_rows, block_cols = region.shape
    regions = jnp.concatenate([region[...].astype(F32), jnp.zeros((8 - block_rows, block_cols), F32)])
    spread = one_hot(iota((cols, block_cols), 0) // 2 == iota((cols, block_cols), 1))
    column_region = matmul_nt(spread, regions.astype(BF16)).astype(BF16)
    plane, lane = iota((planes * rows, LANES), 0), iota((planes * rows, LANES), 1)
    ones = jnp.where((iota((cols, LANES), 1) == ONE_LANE) | (iota((cols, LANES), 1) == ONE_LANE + 1), 1.0, 0.0)
    cells = []
    for r in range(rows):
        place = one_hot((plane == lane * rows + r) | (plane == (lane - LOW_LANE) * rows + r))
        region_place = one_hot((iota((8, LANES), 0) == r // 2) & (iota((8, LANES), 1) == REGION_LANE))
        flags = matmul(column_bits, place) + matmul(column_region, region_place) + ones
        cells.append(jnp.concatenate([state[r * cols : (r + 1) * cols].astype(F32), flags], axis=1))
    write_patch(outs, cells)


def fetch(sources, targets, sems):
    return [pltpu.make_async_copy(*pair, sems.at[i]) for i, pair in enumerate(zip(sources, targets))]


def prepare_kernel(candidate_bits, gate_bits, bias, embed, bit_weight, spread):
    by_bit = jnp.concatenate([candidate_bits[...], gate_bits[...]], axis=1)
    bias = jnp.concatenate([jnp.zeros_like(bias), bias[...]], axis=1)
    lane = iota((LANES, 1), 0)
    weight = jnp.zeros(bit_weight.shape, F32)
    for part in range(2):
        begin = (0, LOW_LANE)[part]
        for bit in range(2):
            row = two_parts(by_bit[bit : bit + 1])[part].astype(F32)
            here = (lane >= begin) & (lane < begin + 2 * ROUNDS) & (lane % 2 == bit)
            weight = jnp.where(here, row, weight)
        weight = jnp.where(lane == ONE_LANE + part, two_parts(bias)[part].astype(F32), weight)
    bit_weight[...] = weight.astype(BF16)
    for at in range(0, spread.shape[0], embed.shape[0]):
        spread[at : at + embed.shape[0]] = embed[...]


class Patch:
    def __init__(self, cols, state, taps, bits, mask):
        self.cols, self.span, self.width = cols, cols + 2 * HALF, HALF
        self.state, self.taps, self.bits, self.mask = state, taps, bits, mask
        self.groups, self.count = state.shape[:2]
        self.rows, self.channels = self.count // self.span, self.groups * LANES

    def get(self, at):
        return jnp.concatenate([self.state[j, at] for j in range(self.groups)], axis=1)

    def put(self, at, values):
        for j in range(self.groups):
            self.state[j, at] = values[:, j * LANES : (j + 1) * LANES]

    def fill(self, parts, halo, put):
        above, below, left, right = halo
        r = 0
        for part, part_rows in (
            (above, self.width), *((part, part.shape[0] // self.cols) for part in parts), (below, self.width)
        ):
            length = part.shape[0] // part_rows
            for at in range(0, part.shape[0], length):
                put(pl.ds(r * self.span + (self.span - length) // 2, length), part[at : at + length].astype(F32))
                r += 1
        for part, first in ((left, 0), (right, self.width + self.cols)):
            values = part[...].astype(F32)
            side_rows = values.shape[0] // self.width
            for r in range(side_rows):
                at = (r + (self.rows - side_rows) // 2) * self.span + first
                put(pl.ds(at, self.width), values[r * self.width : (r + 1) * self.width])

    def keep(self, slot, first, values):
        size = values.shape[0]
        mask = self.mask[first : first + size]
        values = jnp.concatenate([values[:, c : c + LANES] * mask for c in range(0, self.channels, LANES)], axis=1)
        for b in range(3):
            moved = values if b == 1 else pltpu.roll(values, 1 if b == 0 else size - 1, 0)
            self.taps[slot, first : first + size, b * self.channels : (b + 1) * self.channels] = moved.astype(BF16)

    def begin(self):
        part = self.count // 2
        for first in range(0, self.count, part):
            self.keep(0, first, self.get(pl.ds(first, part)))

    def advance(self, first_round, flags, conv, gate_weight, bit_weight, waits):
        span, channels, rows = self.span, self.channels, self.rows
        lane = iota((1, LANES), 1)
        for step in range(HALF):
            t, slot = first_round + step, step % 2
            now = (lane == 2 * t) | (lane == 2 * t + 1) | (lane == LOW_LANE + 2 * t) | (lane == LOW_LANE + 2 * t + 1)
            self.bits[...] = flags[...] * one_hot(now | (lane >= ONE_LANE))
            total = rows - 2 * (step + 1)
            for begin, part_rows in ((step + 1, total),):
                first, size = begin * span, part_rows * span
                parts = [self.taps[slot, first + a * span : first + a * span + size] for a in (-1, 0, 1)]
                flag = self.bits[first : first + size]
                rounded = self.taps[slot, first : first + size, channels : 2 * channels]
                candidate = matmul(flag, bit_weight[:, :channels])
                if step == 0:
                    third = conv.shape[0] // 3
                    for a in range(3):
                        waits[a].wait()
                        candidate = candidate + matmul(parts[a], conv[a * third : (a + 1) * third])
                    waits[3].wait()
                else:
                    candidate = candidate + matmul(jnp.concatenate(parts, axis=1), conv[...])
                gate = matmul(rounded, gate_weight[...]) + matmul(flag, bit_weight[:, channels:])
                before = self.get(pl.ds(first, size))
                after = before + (0.5 * jnp.tanh(0.5 * gate) + 0.5) * (jnp.tanh(candidate) - before)
                self.put(pl.ds(first, size), after)
                if step < HALF - 1:
                    self.keep(1 - slot, first, after)

    def own(self, r):
        return self.get(pl.ds((self.width + r) * self.span + self.width, self.cols))


def patch_scratch(rows, cols, channels):
    count = (rows + 2 * HALF) * (cols + 2 * HALF)
    return [
        pltpu.VMEM((channels // LANES, count, LANES), F32),
        pltpu.VMEM((2, count, 3 * channels), BF16),
        pltpu.VMEM((count, LANES), BF16),
        pltpu.VMEM((count, LANES), F32),
    ]


def mask_of(flags):
    return matmul(flags, one_hot(iota((LANES, LANES), 0) == ONE_LANE))


def thirds(ref):
    size = ref.shape[0] // 3
    return [ref.at[a * size : (a + 1) * size] for a in range(3)]


def first_kernel(cols, place, top, bottom, *refs):
    halo, (region, bit_weight, conv_hbm, gate_hbm) = refs[:4], refs[4:8]
    (exact, kept, given, flags), new_patch = refs[8:12], refs[12:16]
    state, taps, bits, mask, flags_wide, conv, gate_weight, sems = refs[16:]
    copies = fetch((*thirds(conv_hbm), gate_hbm), (*thirds(conv), gate_weight), sems)
    for copy in copies:
        copy.start()
    patch = Patch(cols, state, taps, bits, mask)
    channels = patch.channels

    def put(at, values):
        patch.put(at, values[:, :channels])
        flags_wide[at] = values[:, channels:]

    patch.fill((top, bottom), halo, put)
    flags[...] = flags_wide[...].astype(BF16)
    mask[...] = mask_of(flags[...])
    patch.begin()
    patch.advance(0, flags, conv, gate_weight, bit_weight, copies)

    own = patch.rows - 2 * patch.width
    cells = [patch.own(r) for r in range(own)]
    for r in range(own):
        exact[r * cols : (r + 1) * cols] = cells[r]
    write_patch(new_patch, cells)
    block_cols = cols // 2
    half = kept.shape[0]
    total = jnp.zeros((2 * half, channels), F32)
    for r in range(0, own, 2):
        begin = (patch.width + r) * patch.span + patch.width
        parts = [
            patch.get(pl.ds(begin + a * patch.span + b, block_cols, stride=2)) for a in range(2) for b in range(2)
        ]
        pooled = (sum(parts[1:], parts[0]) * 0.25).astype(BF16)
        member = one_hot(iota((2 * half, block_cols), 0) == region[r // 2 : r // 2 + 1])
        total = total + matmul(member, pooled)
    is_first = place[1] == 0
    kept[...] = jnp.where(is_first, total[:half], total[half:])
    given[...] = jnp.where(is_first, total[half:], total[:half]).astype(BF16)


def repeat_into(out, values):
    count = values.shape[0]
    for at in range(0, out.shape[0], count):
        out[at : at + count] = values.astype(BF16)


def pair_kernel(kept, received, out):
    repeat_into(out, kept[...] + received[...].astype(F32))


def band_kernel(chips, pieces, out):
    values = pieces[...].astype(F32)
    count = values.shape[0] // chips
    parts = [values[p * count : (p + 1) * count] for p in range(chips)]
    repeat_into(out, sum(parts[1:], parts[0]))


def second_kernel(cols, bands, place, sums, other_sums, attn_gain, mlp_gain, *refs):
    sources, (state_out, context_out) = refs[:18], refs[18:20]
    state, taps, bits, mask, sums_all, tokens_all, normed_all, keys, values, member, tokens, normed = refs[20:32]
    attention, hidden, context, sems = refs[32:36]
    targets = refs[36:]
    embed, flags, exact, above, below, left, right, bit_weight = targets[1:9]
    pool_weight, key_weight, value_weight, query_weight = targets[0], *targets[9:12]
    out_weight, up_weight, down_weight, return_weight, gate_weight, conv = targets[12:]
    copies = fetch((*sources[:-1], *thirds(sources[-1])), (*targets[:-1], *thirds(conv)), sems)
    patch = Patch(cols, state, taps, bits, mask)
    own_half = place[1]

    def start(*numbers):
        for number in numbers:
            copies[number].start()

    start(0, 1, 2, 9)

    half_tokens = sums.shape[0] // bands
    band_tokens = 2 * half_tokens
    for band in range(bands):
        at = pl.ds(band * half_tokens, half_tokens)
        pair = sums[at].astype(F32), other_sums[at].astype(F32)
        for half in range(2):
            part = jnp.where(own_half == half, *pair).astype(BF16)
            sums_all[pl.ds(band * band_tokens + half * half_tokens, half_tokens)] = part
    copies[0].wait()
    copies[1].wait()
    start(10, 11)
    total = embed[...].astype(F32) + matmul(sums_all[...], pool_weight[...])
    tokens_all[...] = total
    normed_all[...] = rms_norm(total, attn_gain[...]).astype(BF16)

    copies[2].wait()
    mask[...] = mask_of(flags[...])
    region = matmul(flags[...], one_hot(iota((LANES, LANES), 0) == REGION_LANE))
    member[...] = jnp.where(region == iota(region.shape, 1).astype(F32), 1.0, 0.0)

    g = place[0]
    own = pl.ds(pl.multiple_of(g * band_tokens, band_tokens), band_tokens)
    tokens[:band_tokens] = tokens_all[own]
    normed[:band_tokens] = normed_all[own]
    blocks = patch.span // 2
    room = (blocks + 7) // 8 * 8
    block_rows = patch.width // 2
    side = room * block_rows
    for number, (band, row) in enumerate(
        ((jnp.maximum(g - 1, 0), 0), (jnp.minimum(g + 1, bands - 1), patch.rows - patch.width))
    ):
        pick = jnp.concatenate(
            [member[pl.ds((row + 2 * r) * patch.span, room, stride=2)] for r in range(block_rows)]
        ).astype(BF16)
        at = pl.ds(pl.multiple_of(band * band_tokens, band_tokens), band_tokens)
        into = pl.ds(band_tokens + number * side, side)
        tokens[into] = select(pick, tokens_all[at])
        normed[into] = matmul(pick, normed_all[at]).astype(BF16)

    copies[9].wait()
    start(12, 13)
    keys[...] = matmul(normed_all[...], key_weight[...]).astype(BF16)
    copies[10].wait()
    start(14, 15)
    values[...] = matmul(normed_all[...], value_weight[...]).astype(BF16)
    copies[11].wait()
    start(*range(3, 9))
    queries = matmul(normed[...], query_weight[...]).astype(BF16)
    for head in range(HEADS):
        at = slice(head * HDIM, (head + 1) * HDIM)
        scores = matmul_nt(queries[:, at], keys[:, at]) * (1.0 / math.sqrt(HDIM))
        weights = jnp.exp(scores - jnp.max(scores, axis=-1, keepdims=True))
        denominator = jnp.sum(weights, axis=-1, keepdims=True)
        attention[:, at] = (matmul(weights.astype(BF16), values[:, at]) / denominator).astype(BF16)
    copies[12].wait()
    start(*range(16, len(copies)))
    attended = tokens[...] + matmul(attention[...], out_weight[...])
    tokens[...] = attended
    normed[...] = rms_norm(attended, mlp_gain[...]).astype(BF16)
    copies[13].wait()
    part = 512
    for at in range(0, up_weight.shape[1], part):
        hidden[:, at : at + part] = jax.nn.gelu(matmul(normed[...], up_weight[:, at : at + part])).astype(BF16)
    copies[14].wait()
    context[...] = (tokens[...] + matmul(hidden[...], down_weight[...])).astype(BF16)
    context_out[...] = context[:band_tokens]
    copies[15].wait()
    returned = matmul(context[...], return_weight[...])

    for copy in copies[3:9]:
        copy.wait()
    patch.fill((exact,), (above, below, left, right), patch.put)
    first, last = patch.width * patch.span, (patch.rows - patch.width) * patch.span
    middle = pl.ds(first, last - first)
    patch.put(middle, patch.get(middle) + select(member[first:last].astype(BF16), returned[:band_tokens]))
    for number, row in enumerate((0, patch.rows - patch.width)):
        for r in range(patch.width):
            start = band_tokens + number * side + r // 2 * room
            share = returned[start : start + blocks]
            for c in range(2):
                at = pl.ds((row + r) * patch.span + c, blocks, stride=2)
                patch.put(at, patch.get(at) + share)

    patch.begin()
    patch.advance(HALF, flags, conv, gate_weight, bit_weight, (*copies[17:], copies[16]))
    for r in range(patch.rows - 2 * patch.width):
        state_out[r * cols : (r + 1) * cols] = patch.own(r).astype(BF16)


def local(
    syndrome_bits, region_assign, state_in, bit_to_candidate, bit_to_gate, conv_weight, gate_weight, gate_bias,
    pool_weight, region_embed, attn_norm_gain, query_weight, key_weight, value_weight, out_weight, mlp_norm_gain,
    mlp_up, mlp_down, return_weight,
):
    rows, cols, channels = state_in.shape
    band_tokens, embed_width = region_embed.shape
    bands, tiles = lax.axis_size("ctx"), math.prod(lax.axis_size(name) for name in TILE)
    conv = conv_weight.reshape(9 * channels, channels)
    place = jnp.stack([lax.axis_index("ctx"), lax.axis_index("core")]).astype(jnp.int32)
    swap = [(0, 1), (1, 0)]
    half = HALF * cols

    top, bottom, first, last = call(
        message_kernel,
        "message",
        (syndrome_bits.reshape(2 * ROUNDS, rows, cols), region_assign, state_in.reshape(rows * cols, channels)),
        patch_outputs(half, channels + LANES),
        grant=8,
    )
    above, below = row_halo(top, bottom)
    embed, _ = lax.optimization_barrier((region_embed, top))
    bit_weight, embed = call(
        prepare_kernel,
        "prepare",
        (bit_to_candidate, bit_to_gate, gate_bias[None], embed),
        [array(LANES, 2 * channels, BF16), array(bands * band_tokens, embed_width, BF16)],
        moved=8 * MIB,
    )
    embed, bit_weight, above, below = lax.optimization_barrier((embed, bit_weight, above, below))
    left, right = col_halo(cols, above, first, last, below)
    embed = lax.all_to_all(embed.reshape(bands, band_tokens, -1), "ctx", 0, 0).reshape(-1, embed_width)

    count = (rows + 2 * HALF) * (cols + 2 * HALF)
    flops = 15 * rows * cols * HALF * 2 * channels * channels
    exact, kept, given, flags, top, bottom, first, last = call(
        functools.partial(first_kernel, cols),
        "rounds",
        (place, top, bottom, above, below, left, right, region_assign, bit_weight, conv, gate_weight),
        [
            array(rows * cols, channels, F32), array(band_tokens // 2, channels, F32),
            array(band_tokens // 2, channels, BF16), array(count, LANES, BF16),
        ]
        + patch_outputs(half, channels),
        patch_scratch(rows, cols, channels)
        + [
            pltpu.VMEM((count, LANES), F32), pltpu.VMEM(conv.shape, BF16), pltpu.VMEM(gate_weight.shape, BF16),
            pltpu.SemaphoreType.DMA((4,)),
        ],
        in_hbm=(9, 10),
        scalars=(0,),
        flops=flops,
    )

    chips, half_tokens = tiles // 2, band_tokens // 2
    given, embed = lax.optimization_barrier((given, embed))
    received = lax.ppermute(given, "core", swap)
    (pieces,) = call(
        pair_kernel, "pair", (kept, received), [array(chips * half_tokens, channels, BF16)], grant=8
    )
    pieces = lax.all_to_all(pieces.reshape(chips, half_tokens, channels), "chip", 0, 0)
    above, below = row_halo(top, bottom)
    pieces, above, below = lax.optimization_barrier((pieces, above, below))
    (sums,) = call(
        functools.partial(band_kernel, chips),
        "band",
        (pieces.reshape(-1, channels),),
        [array(bands * half_tokens, channels, BF16)],
        grant=8,
    )
    above, below, sums = lax.optimization_barrier((above, below, sums))
    sums = lax.all_to_all(sums.reshape(bands, half_tokens, channels), "ctx", 0, 0)
    left, right = col_halo(cols, above, first, last, below)
    sums, left, right = lax.optimization_barrier((sums.reshape(-1, channels), left, right))
    other_sums = lax.ppermute(sums, "core", swap)

    fetched = (
        pool_weight, embed, flags, exact, above, below, left, right, bit_weight, key_weight, value_weight, query_weight,
        out_weight, mlp_up, mlp_down, return_weight, gate_weight, conv,
    )
    blocks = (cols + 2 * HALF) // 2
    layer_rows = band_tokens + HALF * ((blocks + 7) // 8 * 8)
    all_tokens = bands * band_tokens
    state, context = call(
        functools.partial(second_kernel, cols, bands),
        "context",
        (place, sums, other_sums, attn_norm_gain[None], mlp_norm_gain[None], *fetched),
        [array(rows * cols, channels, BF16), array(band_tokens, embed_width, BF16)],
        patch_scratch(rows, cols, channels)
        + [
            pltpu.VMEM((all_tokens, channels), BF16),
            pltpu.VMEM((all_tokens, embed_width), F32), pltpu.VMEM((all_tokens, embed_width), BF16),
            pltpu.VMEM((all_tokens, embed_width), BF16), pltpu.VMEM((all_tokens, embed_width), BF16),
            pltpu.VMEM((count, LANES), F32),
            pltpu.VMEM((layer_rows, embed_width), F32), pltpu.VMEM((layer_rows, embed_width), BF16),
            pltpu.VMEM((layer_rows, embed_width), BF16), pltpu.VMEM((layer_rows, mlp_up.shape[1]), BF16),
            pltpu.VMEM((layer_rows, embed_width), BF16), pltpu.SemaphoreType.DMA((len(fetched) + 2,)),
        ]
        + [pltpu.VMEM(value.shape, value.dtype) for value in fetched],
        in_hbm=range(5, 5 + len(fetched)),
        scalars=(0,),
        flops=2 * flops,
    )
    return (state.reshape(rows, cols, channels), context)


def solution(mesh):
    bands, tiles = mesh.devices.shape
    split = jax.sharding.Mesh(mesh.devices.reshape(bands, tiles // 2, 2), ("ctx", *TILE))
    return jax.shard_map(
        local,
        mesh=split,
        in_specs=(
            P(None, None, "ctx", TILE),
            P("ctx", TILE),
            P("ctx", TILE, None),
            P(), P(), P(), P(), P(), P(),
            P("ctx", None),
            P(), P(), P(), P(), P(), P(), P(), P(), P(),
        ),
        out_specs=(P("ctx", TILE, None), P("ctx", None)),
        check_vma=False,
    )
```

profile of v0, /device:TPU:0, one launch (start us, length us, event | category | flops | bytes accessed | tf_op | source)
XLA Modules:
  0.0 109.3 jit_solution(2549645728588439914)
XLA Ops:
  0.6 0.0 copy-start
  0.6 0.9 copy-done
  1.6 0.0 copy-start.6
  1.6 0.8 copy-done.6
  2.4 0.0 copy-start.9
  2.4 0.7 copy-done.9
  3.1 0.3 message.1
  3.4 0.0 copy-start.10
  3.5 0.0 copy-start.11
  3.5 4.9 %collective-permute-start = (bf16[128,640]{1,0:T(8,128)(2,1)S(1)}, bf16[128,640]{1,0:T(8,128)(2,1)S(1)}, u32[]{:S(2)}, u32[]{:S(2)}) collective-permute-start(bf16[128,640]{1,0:T(8,128)(2,1)S(1)} %get-tuple-element.39.bottom), channel_id=1, source_target_pairs={{0,8},{8,16},{16,24},{1,9},{9,17},{17,25},{2,10},{10,18},{18,26},{... | collective-permute-start | bytes 491528 | tf_op jit(solution)/shard_map/ppermute | solution.py:28
  8.3 1.3 %collective-permute-start.1 = (bf16[128,640]{1,0:T(8,128)(2,1)S(1)}, bf16[128,640]{1,0:T(8,128)(2,1)S(1)}, u32[]{:S(2)}, u32[]{:S(2)}) collective-permute-start(bf16[128,640]{1,0:T(8,128)(2,1)S(1)} %get-tuple-element.38.top), channel_id=1, source_target_pairs={{8,0},{16,8},{24,16},{9,1},{17,9},{25,17},{10,2},{18,10},{26,18},{... | collective-permute-start | bytes 491528 | tf_op jit(solution)/shard_map/ppermute | solution.py:28
  9.6 2.2 %prepare.1 = (bf16[128,1024]{1,0:T(8,128)(2,1)}, bf16[512,1024]{1,0:T(8,128)(2,1)}) custom-call(f32[2,512]{1,0:T(2,128)} %candidate_bits.1, f32[2,512]{1,0:T(2,128)} %gate_bits.1, f32[1,512]{1,0:T(1,128)} %bitcast.22, bf16[128,1024]{1,0:T(8,128)(2,1)} %embed), custom_call_target="tpu_custom_call" | custom-call | bytes 8388608 | tf_op jit(solution)/shard_map/prepare/pallas_call | solution.py:83
  11.8 0.0 collective-permute-done.above.refs_0_
  11.8 0.0 copy-start.1
  11.8 5.4 %collective-permute-done.1.below.refs_1_ = bf16[128,640]{1,0:T(8,128)(2,1)S(1)} collective-permute-done((bf16[128,640]{1,0:T(8,128)(2,1)S(1)}, bf16[128,640]{1,0:T(8,128)(2,1)S(1)}, u32[]{:S(2)}, u32[]{:S(2)}) %collective-permute-start.1) | collective-permute-done | bytes 163872 | tf_op jit(solution)/shard_map/ppermute | solution.py:28
  17.2 0.0 copy-start.2
  17.2 3.5 %all-to-all-start = ((bf16[4,128,1024]{2,1,0:T(8,128)(2,1)}), bf16[4,128,1024]{2,1,0:T(8,128)(2,1)S(1)}, u32[]{:S(2)}, u32[]{:S(2)}) async-start(bf16[4,128,1024]{2,1,0:T(8,128)(2,1)} %bitcast.19), calls=%async_computation | async-start | bytes 2097152 | tf_op jit(solution)/shard_map/all_to_all | solution.py:456
  20.8 1.3 %collective-permute-start.2 = (bf16[64,640]{1,0:T(8,128)(2,1)S(1)}, bf16[64,640]{1,0:T(8,128)(2,1)S(1)}, u32[]{:S(2)}, u32[]{:S(2)}) collective-permute-start(bf16[64,640]{1,0:T(8,128)(2,1)S(1)} %get-tuple-element.47), channel_id=1, source_target_pairs={{0,1},{1,2},{2,3},{3,4},{4,5},{5,6},{6,7},{8,9},{9,10},{10,11},{11... | collective-permute-start | bytes 245768 | tf_op jit(solution)/shard_map/ppermute | solution.py:28
  22.1 1.3 %collective-permute-start.3 = (bf16[64,640]{1,0:T(8,128)(2,1)S(1)}, bf16[64,640]{1,0:T(8,128)(2,1)S(1)}, u32[]{:S(2)}, u32[]{:S(2)}) collective-permute-start(bf16[64,640]{1,0:T(8,128)(2,1)S(1)} %get-tuple-element.48), channel_id=1, source_target_pairs={{1,0},{2,1},{3,2},{4,3},{5,4},{6,5},{7,6},{9,8},{10,9},{11,10},{12... | collective-permute-start | bytes 245768 | tf_op jit(solution)/shard_map/ppermute | solution.py:28
  23.4 0.7 pad_add_fusion.place
  24.1 0.0 collective-permute-done.2.refs_2_
  24.1 0.0 copy-start.15
  24.1 3.0 %collective-permute-done.3.refs_3_ = bf16[64,640]{1,0:T(8,128)(2,1)S(1)} collective-permute-done((bf16[64,640]{1,0:T(8,128)(2,1)S(1)}, bf16[64,640]{1,0:T(8,128)(2,1)S(1)}, u32[]{:S(2)}, u32[]{:S(2)}) %collective-permute-start.3) | collective-permute-done | bytes 81952 | tf_op jit(solution)/shard_map/ppermute | solution.py:28
  27.1 0.0 copy-start.16
  27.1 0.0 copy-done.10
  27.1 0.0 copy-done.11
  27.1 0.0 copy-done.1
  27.1 0.0 copy-done.2
  27.1 0.0 copy-done.15
  27.1 0.6 copy-done.16
  27.7 15.5 %rounds.1 = (f32[256,512]{1,0:T(8,128)}, f32[64,512]{1,0:T(8,128)}, bf16[64,512]{1,0:T(8,128)(2,1)}, bf16[640,128]{1,0:T(8,128)(2,1)}, bf16[128,512]{1,0:T(8,128...) custom-call(s32[2]{0:T(128)} %pad_add_fusion.place, ...), custom_call_target="tpu_custom_call" | custom-call | flops 8053063680 | bytes 1048576 | tf_op jit(solution)/shard_map/rounds/pallas_call | solution.py:83
  43.2 0.0 all-to-all-done
  43.2 0.0 copy-start.12
  43.3 3.4 %collective-permute-start.4 = (bf16[64,512]{1,0:T(8,128)(2,1)}, bf16[64,512]{1,0:T(8,128)(2,1)S(1)}, u32[]{:S(2)}, u32[]{:S(2)}) collective-permute-start(bf16[64,512]{1,0:T(8,128)(2,1)} %get-tuple-element.53), channel_id=1, source_target_pairs={{0,1},{1,0},{2,3},{3,2},{4,5},{5,4},{6,7},{7,6},{8,9},{9,8},{10,11... | collective-permute-start | bytes 196616 | tf_op jit(solution)/shard_map/ppermute | solution.py:481
  46.7 1.1 %collective-permute-done.4.received = bf16[64,512]{1,0:T(8,128)(2,1)S(1)} collective-permute-done((bf16[64,512]{1,0:T(8,128)(2,1)}, bf16[64,512]{1,0:T(8,128)(2,1)S(1)}, u32[]{:S(2)}, u32[]{:S(2)}) %collective-permute-start.4) | collective-permute-done | bytes 65568 | tf_op jit(solution)/shard_map/ppermute | solution.py:481
  47.8 0.9 copy-done.3
  48.7 0.7 pair.1
  49.4 3.9 %all-to-all-start.1 = ((bf16[4,64,512]{2,1,0:T(8,128)(2,1)}), bf16[4,64,512]{2,1,0:T(8,128)(2,1)S(1)}, u32[]{:S(2)}, u32[]{:S(2)}) async-start(bf16[4,64,512]{2,1,0:T(8,128)(2,1)} %bitcast.8), calls=%async_computation.1 | async-start | bytes 524288 | tf_op jit(solution)/shard_map/all_to_all | solution.py:485
  53.3 3.9 %collective-permute-start.5 = (bf16[128,512]{1,0:T(8,128)(2,1)}, bf16[128,512]{1,0:T(8,128)(2,1)S(1)}, u32[]{:S(2)}, u32[]{:S(2)}) collective-permute-start(bf16[128,512]{1,0:T(8,128)(2,1)} %get-tuple-element.54), channel_id=1, source_target_pairs={{0,8},{8,16},{16,24},{1,9},{9,17},{17,25},{2,10},{10,18},{18,26},{... | collective-permute-start | bytes 393224 | tf_op jit(solution)/shard_map/ppermute | solution.py:28
  57.2 1.3 %collective-permute-start.6 = (bf16[128,512]{1,0:T(8,128)(2,1)}, bf16[128,512]{1,0:T(8,128)(2,1)S(1)}, u32[]{:S(2)}, u32[]{:S(2)}) collective-permute-start(bf16[128,512]{1,0:T(8,128)(2,1)} %get-tuple-element.55), channel_id=1, source_target_pairs={{8,0},{16,8},{24,16},{9,1},{17,9},{25,17},{10,2},{18,10},{26,18},{... | collective-permute-start | bytes 393224 | tf_op jit(solution)/shard_map/ppermute | solution.py:28
  58.5 2.0 %collective-permute-done.5.above.refs_4_ = bf16[128,512]{1,0:T(8,128)(2,1)S(1)} collective-permute-done((bf16[128,512]{1,0:T(8,128)(2,1)}, bf16[128,512]{1,0:T(8,128)(2,1)S(1)}, u32[]{:S(2)}, u32[]{:S(2)}) %collective-permute-start.5) | collective-permute-done | bytes 131104 | tf_op jit(solution)/shard_map/ppermute | solution.py:28
  60.5 4.6 %collective-permute-done.6.below.refs_5_ = bf16[128,512]{1,0:T(8,128)(2,1)S(1)} collective-permute-done((bf16[128,512]{1,0:T(8,128)(2,1)}, bf16[128,512]{1,0:T(8,128)(2,1)S(1)}, u32[]{:S(2)}, u32[]{:S(2)}) %collective-permute-start.6) | collective-permute-done | bytes 131104 | tf_op jit(solution)/shard_map/ppermute | solution.py:28
  65.1 0.0 all-to-all-done.1
  65.1 0.7 band.1
  65.8 3.4 %all-to-all-start.2 = ((bf16[4,64,512]{2,1,0:T(8,128)(2,1)}), bf16[4,64,512]{2,1,0:T(8,128)(2,1)S(1)}, u32[]{:S(2)}, u32[]{:S(2)}) async-start(bf16[4,64,512]{2,1,0:T(8,128)(2,1)} %bitcast.10), calls=%async_computation.2 | async-start | bytes 524288 | tf_op jit(solution)/shard_map/all_to_all | solution.py:496
  69.3 0.0 copy-start.7
  69.3 0.7 copy-done.7
  70.0 0.8 copy-done.8
  70.8 1.4 %collective-permute-start.7 = (bf16[64,512]{1,0:T(8,128)(2,1)S(1)}, bf16[64,512]{1,0:T(8,128)(2,1)S(1)}, u32[]{:S(2)}, u32[]{:S(2)}) collective-permute-start(bf16[64,512]{1,0:T(8,128)(2,1)S(1)} %get-tuple-element.64), channel_id=1, source_target_pairs={{0,1},{1,2},{2,3},{3,4},{4,5},{5,6},{6,7},{8,9},{9,10},{10,11},{11... | collective-permute-start | bytes 196616 | tf_op jit(solution)/shard_map/ppermute | solution.py:28
  72.2 1.5 %collective-permute-start.8 = (bf16[64,512]{1,0:T(8,128)(2,1)S(1)}, bf16[64,512]{1,0:T(8,128)(2,1)S(1)}, u32[]{:S(2)}, u32[]{:S(2)}) collective-permute-start(bf16[64,512]{1,0:T(8,128)(2,1)S(1)} %get-tuple-element.65), channel_id=1, source_target_pairs={{1,0},{2,1},{3,2},{4,3},{5,4},{6,5},{7,6},{9,8},{10,9},{11,10},{12... | collective-permute-start | bytes 196616 | tf_op jit(solution)/shard_map/ppermute | solution.py:28
  73.7 0.0 collective-permute-done.7.refs_6_
  73.7 0.0 copy-start.17
  73.7 3.5 %collective-permute-done.8.refs_7_ = bf16[64,512]{1,0:T(8,128)(2,1)S(1)} collective-permute-done((bf16[64,512]{1,0:T(8,128)(2,1)S(1)}, bf16[64,512]{1,0:T(8,128)(2,1)S(1)}, u32[]{:S(2)}, u32[]{:S(2)}) %collective-permute-start.8) | collective-permute-done | bytes 65568 | tf_op jit(solution)/shard_map/ppermute | solution.py:28
  77.2 0.0 all-to-all-done.2
  77.2 3.0 %collective-permute-start.9 = (bf16[256,512]{1,0:T(8,128)(2,1)S(1)}, bf16[256,512]{1,0:T(8,128)(2,1)S(1)}, u32[]{:S(2)}, u32[]{:S(2)}) collective-permute-start(bf16[256,512]{1,0:T(8,128)(2,1)S(1)} %bitcast.20), channel_id=1, source_target_pairs={{0,1},{1,0},{2,3},{3,2},{4,5},{5,4},{6,7},{7,6},{8,9},{9,8},{10,11... | collective-permute-start | bytes 786440 | tf_op jit(solution)/shard_map/ppermute | solution.py:499
  80.2 1.2 %collective-permute-done.9.other_sums = bf16[256,512]{1,0:T(8,128)(2,1)S(1)} collective-permute-done((bf16[256,512]{1,0:T(8,128)(2,1)S(1)}, bf16[256,512]{1,0:T(8,128)(2,1)S(1)}, u32[]{:S(2)}, u32[]{:S(2)}) %collective-permute-start.9) | collective-permute-done | bytes 262176 | tf_op jit(solution)/shard_map/ppermute | solution.py:499
  81.4 0.0 copy-done.12
  81.4 0.0 copy-done.4
  81.4 0.0 copy-done.5
  81.4 0.0 copy-done.17
  81.4 0.0 copy-done.18
  81.4 0.0 copy-done.13
  81.4 0.7 copy-done.14
  82.1 27.0 %context.1 = (bf16[256,512]{1,0:T(8,128)(2,1)}, bf16[128,1024]{1,0:T(8,128)(2,1)}) custom-call(s32[2]{0:T(128)} %pad_add_fusion.place, bf16[256,512]{1,0:T(8,128)(2,1)} %bitcast.21, bf16[256,512]{1,0:T(8,128)(2,1)} %copy-done.14, f32[1,1024]{1,0:T(1,128)} %bitcast.25, f32[1,1024]{1,0:T(1,128)} %bitcast.26, bf16[512,1024]{1,0:T(8,128)(2,1)} %refs_0_.1, ...), custom_call_target="tpu_custom_call" | custom-call | flops 16106127360 | bytes 1048576 | tf_op jit(solution)/shard_map/context/pallas_call | solution.py:83
  (9 shorter events, 0.1 us)
Async XLA Ops:
  0.6 1.0 copy-start
  1.6 0.8 copy-start.6
  2.4 0.7 copy-start.9
  3.4 23.6 %copy-start.10 = (bf16[128,640]{1,0:T(8,128)(2,1)}, bf16[128,640]{1,0:T(8,128)(2,1)S(1)}, u32[]{:S(2)}) copy-start(bf16[128,640]{1,0:T(8,128)(2,1)S(1)} %get-tuple-element.38.top) | copy-start | bytes 491524
  3.5 23.6 %copy-start.11 = (bf16[128,640]{1,0:T(8,128)(2,1)}, bf16[128,640]{1,0:T(8,128)(2,1)S(1)}, u32[]{:S(2)}) copy-start(bf16[128,640]{1,0:T(8,128)(2,1)S(1)} %get-tuple-element.39.bottom) | copy-start | bytes 491524
  3.5 8.3 %collective-permute-start = (bf16[128,640]{1,0:T(8,128)(2,1)S(1)}, bf16[128,640]{1,0:T(8,128)(2,1)S(1)}, u32[]{:S(2)}, u32[]{:S(2)}) collective-permute-start(bf16[128,640]{1,0:T(8,128)(2,1)S(1)} %get-tuple-element.39.bottom), channel_id=1, source_target_pairs={{0,8},{8,16},{16,24},{1,9},{9,17},{17,25},{2,10},{10,18},{18,26},{... | collective-permute-start | bytes 491528 | tf_op jit(solution)/shard_map/ppermute | solution.py:28
  8.3 8.9 %collective-permute-start.1 = (bf16[128,640]{1,0:T(8,128)(2,1)S(1)}, bf16[128,640]{1,0:T(8,128)(2,1)S(1)}, u32[]{:S(2)}, u32[]{:S(2)}) collective-permute-start(bf16[128,640]{1,0:T(8,128)(2,1)S(1)} %get-tuple-element.38.top), channel_id=1, source_target_pairs={{8,0},{16,8},{24,16},{9,1},{17,9},{25,17},{10,2},{18,10},{26,18},{... | collective-permute-start | bytes 491528 | tf_op jit(solution)/shard_map/ppermute | solution.py:28
  11.8 15.3 %copy-start.1 = (bf16[128,640]{1,0:T(8,128)(2,1)}, bf16[128,640]{1,0:T(8,128)(2,1)S(1)}, u32[]{:S(2)}) copy-start(bf16[128,640]{1,0:T(8,128)(2,1)S(1)} %collective-permute-done.above.refs_0_) | copy-start | bytes 491524
  17.2 9.9 %copy-start.2 = (bf16[128,640]{1,0:T(8,128)(2,1)}, bf16[128,640]{1,0:T(8,128)(2,1)S(1)}, u32[]{:S(2)}) copy-start(bf16[128,640]{1,0:T(8,128)(2,1)S(1)} %collective-permute-done.1.below.refs_1_) | copy-start | bytes 491524
  17.2 26.0 %all-to-all-start = ((bf16[4,128,1024]{2,1,0:T(8,128)(2,1)}), bf16[4,128,1024]{2,1,0:T(8,128)(2,1)S(1)}, u32[]{:S(2)}, u32[]{:S(2)}) async-start(bf16[4,128,1024]{2,1,0:T(8,128)(2,1)} %bitcast.19), calls=%async_computation | async-start | bytes 2097152 | tf_op jit(solution)/shard_map/all_to_all | solution.py:456
  20.8 3.3 %collective-permute-start.2 = (bf16[64,640]{1,0:T(8,128)(2,1)S(1)}, bf16[64,640]{1,0:T(8,128)(2,1)S(1)}, u32[]{:S(2)}, u32[]{:S(2)}) collective-permute-start(bf16[64,640]{1,0:T(8,128)(2,1)S(1)} %get-tuple-element.47), channel_id=1, source_target_pairs={{0,1},{1,2},{2,3},{3,4},{4,5},{5,6},{6,7},{8,9},{9,10},{10,11},{11... | collective-permute-start | bytes 245768 | tf_op jit(solution)/shard_map/ppermute | solution.py:28
  22.1 5.0 %collective-permute-start.3 = (bf16[64,640]{1,0:T(8,128)(2,1)S(1)}, bf16[64,640]{1,0:T(8,128)(2,1)S(1)}, u32[]{:S(2)}, u32[]{:S(2)}) collective-permute-start(bf16[64,640]{1,0:T(8,128)(2,1)S(1)} %get-tuple-element.48), channel_id=1, source_target_pairs={{1,0},{2,1},{3,2},{4,3},{5,4},{6,5},{7,6},{9,8},{10,9},{11,10},{12... | collective-permute-start | bytes 245768 | tf_op jit(solution)/shard_map/ppermute | solution.py:28
  24.1 3.0 %copy-start.15 = (bf16[64,640]{1,0:T(8,128)(2,1)}, bf16[64,640]{1,0:T(8,128)(2,1)S(1)}, u32[]{:S(2)}) copy-start(bf16[64,640]{1,0:T(8,128)(2,1)S(1)} %collective-permute-done.2.refs_2_) | copy-start | bytes 245764
  27.1 0.6 copy-start.16
  43.2 38.1 %copy-start.12 = (bf16[4,128,1024]{2,1,0:T(8,128)(2,1)}, bf16[4,128,1024]{2,1,0:T(8,128)(2,1)S(1)}, u32[]{:S(2)}) copy-start(bf16[4,128,1024]{2,1,0:T(8,128)(2,1)S(1)} %all-to-all-done) | copy-start | bytes 3145732
  43.3 4.6 %collective-permute-start.4 = (bf16[64,512]{1,0:T(8,128)(2,1)}, bf16[64,512]{1,0:T(8,128)(2,1)S(1)}, u32[]{:S(2)}, u32[]{:S(2)}) collective-permute-start(bf16[64,512]{1,0:T(8,128)(2,1)} %get-tuple-element.53), channel_id=1, source_target_pairs={{0,1},{1,0},{2,3},{3,2},{4,5},{5,4},{6,7},{7,6},{8,9},{9,8},{10,11... | collective-permute-start | bytes 196616 | tf_op jit(solution)/shard_map/ppermute | solution.py:481
  47.8 0.9 copy-start.3
  49.4 15.7 %all-to-all-start.1 = ((bf16[4,64,512]{2,1,0:T(8,128)(2,1)}), bf16[4,64,512]{2,1,0:T(8,128)(2,1)S(1)}, u32[]{:S(2)}, u32[]{:S(2)}) async-start(bf16[4,64,512]{2,1,0:T(8,128)(2,1)} %bitcast.8), calls=%async_computation.1 | async-start | bytes 524288 | tf_op jit(solution)/shard_map/all_to_all | solution.py:485
  53.3 7.2 %collective-permute-start.5 = (bf16[128,512]{1,0:T(8,128)(2,1)}, bf16[128,512]{1,0:T(8,128)(2,1)S(1)}, u32[]{:S(2)}, u32[]{:S(2)}) collective-permute-start(bf16[128,512]{1,0:T(8,128)(2,1)} %get-tuple-element.54), channel_id=1, source_target_pairs={{0,8},{8,16},{16,24},{1,9},{9,17},{17,25},{2,10},{10,18},{18,26},{... | collective-permute-start | bytes 393224 | tf_op jit(solution)/shard_map/ppermute | solution.py:28
  57.2 7.9 %collective-permute-start.6 = (bf16[128,512]{1,0:T(8,128)(2,1)}, bf16[128,512]{1,0:T(8,128)(2,1)S(1)}, u32[]{:S(2)}, u32[]{:S(2)}) collective-permute-start(bf16[128,512]{1,0:T(8,128)(2,1)} %get-tuple-element.55), channel_id=1, source_target_pairs={{8,0},{16,8},{24,16},{9,1},{17,9},{25,17},{10,2},{18,10},{26,18},{... | collective-permute-start | bytes 393224 | tf_op jit(solution)/shard_map/ppermute | solution.py:28
  60.5 20.9 %copy-start.4 = (bf16[128,512]{1,0:T(8,128)(2,1)}, bf16[128,512]{1,0:T(8,128)(2,1)S(1)}, u32[]{:S(2)}) copy-start(bf16[128,512]{1,0:T(8,128)(2,1)S(1)} %collective-permute-done.5.above.refs_4_) | copy-start | bytes 393220
  65.1 16.3 %copy-start.5 = (bf16[128,512]{1,0:T(8,128)(2,1)}, bf16[128,512]{1,0:T(8,128)(2,1)S(1)}, u32[]{:S(2)}) copy-start(bf16[128,512]{1,0:T(8,128)(2,1)S(1)} %collective-permute-done.6.below.refs_5_) | copy-start | bytes 393220
  65.8 11.4 %all-to-all-start.2 = ((bf16[4,64,512]{2,1,0:T(8,128)(2,1)}), bf16[4,64,512]{2,1,0:T(8,128)(2,1)S(1)}, u32[]{:S(2)}, u32[]{:S(2)}) async-start(bf16[4,64,512]{2,1,0:T(8,128)(2,1)} %bitcast.10), calls=%async_computation.2 | async-start | bytes 524288 | tf_op jit(solution)/shard_map/all_to_all | solution.py:496
  69.3 0.8 copy-start.7
  70.0 0.8 copy-start.8
  70.8 2.9 %collective-permute-start.7 = (bf16[64,512]{1,0:T(8,128)(2,1)S(1)}, bf16[64,512]{1,0:T(8,128)(2,1)S(1)}, u32[]{:S(2)}, u32[]{:S(2)}) collective-permute-start(bf16[64,512]{1,0:T(8,128)(2,1)S(1)} %get-tuple-element.64), channel_id=1, source_target_pairs={{0,1},{1,2},{2,3},{3,4},{4,5},{5,6},{6,7},{8,9},{9,10},{10,11},{11... | collective-permute-start | bytes 196616 | tf_op jit(solution)/shard_map/ppermute | solution.py:28
  72.2 5.0 %collective-permute-start.8 = (bf16[64,512]{1,0:T(8,128)(2,1)S(1)}, bf16[64,512]{1,0:T(8,128)(2,1)S(1)}, u32[]{:S(2)}, u32[]{:S(2)}) collective-permute-start(bf16[64,512]{1,0:T(8,128)(2,1)S(1)} %get-tuple-element.65), channel_id=1, source_target_pairs={{1,0},{2,1},{3,2},{4,3},{5,4},{6,5},{7,6},{9,8},{10,9},{11,10},{12... | collective-permute-start | bytes 196616 | tf_op jit(solution)/shard_map/ppermute | solution.py:28
  73.7 7.7 %copy-start.17 = (bf16[64,512]{1,0:T(8,128)(2,1)}, bf16[64,512]{1,0:T(8,128)(2,1)S(1)}, u32[]{:S(2)}) copy-start(bf16[64,512]{1,0:T(8,128)(2,1)S(1)} %collective-permute-done.7.refs_6_) | copy-start | bytes 196612
  77.2 4.2 %copy-start.18 = (bf16[64,512]{1,0:T(8,128)(2,1)}, bf16[64,512]{1,0:T(8,128)(2,1)S(1)}, u32[]{:S(2)}) copy-start(bf16[64,512]{1,0:T(8,128)(2,1)S(1)} %collective-permute-done.8.refs_7_) | copy-start | bytes 196612
  77.2 4.2 %copy-start.13 = (bf16[4,64,512]{2,1,0:T(8,128)(2,1)}, bf16[4,64,512]{2,1,0:T(8,128)(2,1)S(1)}, u32[]{:S(2)}) copy-start(bf16[4,64,512]{2,1,0:T(8,128)(2,1)S(1)} %all-to-all-done.2) | copy-start | bytes 786436
  77.2 4.2 %collective-permute-start.9 = (bf16[256,512]{1,0:T(8,128)(2,1)S(1)}, bf16[256,512]{1,0:T(8,128)(2,1)S(1)}, u32[]{:S(2)}, u32[]{:S(2)}) collective-permute-start(bf16[256,512]{1,0:T(8,128)(2,1)S(1)} %bitcast.20), channel_id=1, source_target_pairs={{0,1},{1,0},{2,3},{3,2},{4,5},{5,4},{6,7},{7,6},{8,9},{9,8},{10,11... | collective-permute-start | bytes 786440 | tf_op jit(solution)/shard_map/ppermute | solution.py:499
  81.4 0.7 copy-start.14
where the time goes:
time: 110 us; the launch traced here: 109 us
  Pallas kernels  46.5 us (42%)
  starting transfers between devices  34 us (31%)
  waiting for transfers between devices  20.8 us (19%)
  local copies, waits for them, and re-layouts  6.18 us (6%)
    pallas_call x8, Pallas kernels, call(): pl.pallas_call(kernel, out_shape=outs, in_specs=[spec(index) for index in...  46.5 us
    ppermute x8, waiting for transfers between devices, shifted(): return lax.ppermute(value, axis, pairs)  18.5 us
    ppermute x8, starting transfers between devices, shifted(): return lax.ppermute(value, axis, pairs)  16.8 us
    unnamed x38, local copies, waits for them, and re-layouts  6.18 us
    all_to_all x1, starting transfers between devices, local(): lax.all_to_all(pieces.reshape(chips, half_tokens, channels), 'chip', 0, 0)  3.85 us
    all_to_all x1, starting transfers between devices, local(): lax.all_to_all(embed.reshape(bands, band_tokens, -1), 'ctx', 0, 0)  3.52 us
    ppermute x1, starting transfers between devices, local(): received = lax.ppermute(given, 'core', swap)  3.45 us
    all_to_all x1, starting transfers between devices, local(): lax.all_to_all(sums.reshape(bands, half_tokens, channels), 'ctx', 0, 0)  3.41 us
  transfers between devices with their start and end apart: 13, of which 7 were waited for; matrix products, arithmetic and copies ran while one was open for 1% of the time, Pallas kernels for 16%

commit v1 on v0

--- a/solution.py
+++ b/solution.py
@@ -105,6 +105,18 @@
     for own, begin, out in ((own_first, 0, first), (own_last, cols - HALF, last)):
         parts = first_columns(above, cols, begin) + [own[...].astype(F32)] + first_columns(below, cols, begin)
         out[...] = jnp.concatenate(parts).astype(BF16)
+
+
+def rows_kernel(top, bottom, left, right, up, down):
+    sides = left[...].astype(F32), right[...].astype(F32)
+    cols = top.shape[0] // HALF
+    for number, (part, out) in enumerate(((top, up), (bottom, down))):
+        values, cells = part[...].astype(F32), []
+        for r in range(HALF):
+            at = (number * HALF + r) * HALF
+            before, after = (side[at : at + HALF] for side in sides)
+            cells += [before, values[r * cols : (r + 1) * cols], after]
+        out[...] = jnp.concatenate(cells).astype(BF16)
 
 
 def patch_outputs(half, lanes):
@@ -315,23 +327,21 @@
     repeat_into(out, sum(parts[1:], parts[0]))
 
 
-def second_kernel(cols, bands, place, sums, other_sums, attn_gain, mlp_gain, *refs):
-    sources, (state_out, context_out) = refs[:18], refs[18:20]
-    state, taps, bits, mask, sums_all, tokens_all, normed_all, keys, values, member, tokens, normed = refs[20:32]
-    attention, hidden, context, sems = refs[32:36]
-    targets = refs[36:]
-    embed, flags, exact, above, below, left, right, bit_weight = targets[1:9]
-    pool_weight, key_weight, value_weight, query_weight = targets[0], *targets[9:12]
-    out_weight, up_weight, down_weight, return_weight, gate_weight, conv = targets[12:]
+def second_kernel(
+    cols, bands, place, sums, other_sums, embed, flags, exact, above, below, left, right, attn_gain, mlp_gain, bit_weight,
+    *refs
+):
+    sources, (state_out, context_out), refs = refs[:10], refs[10:12], refs[12:]
+    state, taps, bits, mask, sums_all, tokens_all, normed_all, keys, values, member, tokens, normed = refs[:12]
+    attention, hidden, context, sems = refs[12:16]
+    targets = refs[16:]
+    pool_weight, key_weight, value_weight, query_weight, out_weight = targets[:5]
+    up_weight, down_weight, return_weight, gate_weight, conv = targets[5:]
     copies = fetch((*sources[:-1], *thirds(sources[-1])), (*targets[:-1], *thirds(conv)), sems)
+    for copy in copies:
+        copy.start()
     patch = Patch(cols, state, taps, bits, mask)
     own_half = place[1]
-
-    def start(*numbers):
-        for number in numbers:
-            copies[number].start()
-
-    start(0, 1, 2, 9)
 
     half_tokens = sums.shape[0] // bands
     band_tokens = 2 * half_tokens
@@ -342,13 +352,10 @@
             part = jnp.where(own_half == half, *pair).astype(BF16)
             sums_all[pl.ds(band * band_tokens + half * half_tokens, half_tokens)] = part
     copies[0].wait()
-    copies[1].wait()
-    start(10, 11)
     total = embed[...].astype(F32) + matmul(sums_all[...], pool_weight[...])
     tokens_all[...] = total
     normed_all[...] = rms_norm(total, attn_gain[...]).astype(BF16)
 
-    copies[2].wait()
     mask[...] = mask_of(flags[...])
     region = matmul(flags[...], one_hot(iota((LANES, LANES), 0) == REGION_LANE))
     member[...] = jnp.where(region == iota(region.shape, 1).astype(F32), 1.0, 0.0)
@@ -372,14 +379,11 @@
         tokens[into] = select(pick, tokens_all[at])
         normed[into] = matmul(pick, normed_all[at]).astype(BF16)
 
-    copies[9].wait()
-    start(12, 13)
+    copies[1].wait()
     keys[...] = matmul(normed_all[...], key_weight[...]).astype(BF16)
-    copies[10].wait()
-    start(14, 15)
+    copies[2].wait()
     values[...] = matmul(normed_all[...], value_weight[...]).astype(BF16)
-    copies[11].wait()
-    start(*range(3, 9))
+    copies[3].wait()
     queries = matmul(normed[...], query_weight[...]).astype(BF16)
     for head in range(HEADS):
         at = slice(head * HDIM, (head + 1) * HDIM)
@@ -387,23 +391,20 @@
         weights = jnp.exp(scores - jnp.max(scores, axis=-1, keepdims=True))
         denominator = jnp.sum(weights, axis=-1, keepdims=True)
         attention[:, at] = (matmul(weights.astype(BF16), values[:, at]) / denominator).astype(BF16)
-    copies[12].wait()
-    start(*range(16, len(copies)))
+    copies[4].wait()
     attended = tokens[...] + matmul(attention[...], out_weight[...])
     tokens[...] = attended
     normed[...] = rms_norm(attended, mlp_gain[...]).astype(BF16)
-    copies[13].wait()
+    copies[5].wait()
     part = 512
     for at in range(0, up_weight.shape[1], part):
         hidden[:, at : at + part] = jax.nn.gelu(matmul(normed[...], up_weight[:, at : at + part])).astype(BF16)
-    copies[14].wait()
+    copies[6].wait()
     context[...] = (tokens[...] + matmul(hidden[...], down_weight[...])).astype(BF16)
     context_out[...] = context[:band_tokens]
-    copies[15].wait()
+    copies[7].wait()
     returned = matmul(context[...], return_weight[...])
 
-    for copy in copies[3:9]:
-        copy.wait()
     patch.fill((exact,), (above, below, left, right), patch.put)
     first, last = patch.width * patch.span, (patch.rows - patch.width) * patch.span
     middle = pl.ds(first, last - first)
@@ -417,7 +418,7 @@
                 patch.put(at, patch.get(at) + share)
 
     patch.begin()
-    patch.advance(HALF, flags, conv, gate_weight, bit_weight, (*copies[17:], copies[16]))
+    patch.advance(HALF, flags, conv, gate_weight, bit_weight, (*copies[9:], copies[8]))
     for r in range(patch.rows - 2 * patch.width):
         state_out[r * cols : (r + 1) * cols] = patch.own(r).astype(BF16)
 
@@ -451,7 +452,7 @@
         [array(LANES, 2 * channels, BF16), array(bands * band_tokens, embed_width, BF16)],
         moved=8 * MIB,
     )
-    embed, bit_weight, above, below = lax.optimization_barrier((embed, bit_weight, above, below))
+    embed, bit_weight, above, below, place = lax.optimization_barrier((embed, bit_weight, above, below, place))
     left, right = col_halo(cols, above, first, last, below)
     embed = lax.all_to_all(embed.reshape(bands, band_tokens, -1), "ctx", 0, 0).reshape(-1, embed_width)
 
@@ -483,8 +484,15 @@
         pair_kernel, "pair", (kept, received), [array(chips * half_tokens, channels, BF16)], grant=8
     )
     pieces = lax.all_to_all(pieces.reshape(chips, half_tokens, channels), "chip", 0, 0)
-    above, below = row_halo(top, bottom)
-    pieces, above, below = lax.optimization_barrier((pieces, above, below))
+    left, right = shifted(last, TILE, 1), shifted(first, TILE, -1)
+    up, down = call(
+        rows_kernel,
+        "rows",
+        (top, bottom, left, right),
+        [array(HALF * (cols + 2 * HALF), channels, BF16)] * 2,
+        grant=8,
+    )
+    pieces, up, down = lax.optimization_barrier((pieces, up, down))
     (sums,) = call(
         functools.partial(band_kernel, chips),
         "band",
@@ -492,15 +500,15 @@
         [array(bands * half_tokens, channels, BF16)],
         grant=8,
     )
-    above, below, sums = lax.optimization_barrier((above, below, sums))
+    up, down, sums = lax.optimization_barrier((up, down, sums))
     sums = lax.all_to_all(sums.reshape(bands, half_tokens, channels), "ctx", 0, 0)
-    left, right = col_halo(cols, above, first, last, below)
-    sums, left, right = lax.optimization_barrier((sums.reshape(-1, channels), left, right))
+    above, below = row_halo(up, down)
+    sums, above, below = lax.optimization_barrier((sums.reshape(-1, channels), above, below))
     other_sums = lax.ppermute(sums, "core", swap)
 
     fetched = (
-        pool_weight, embed, flags, exact, above, below, left, right, bit_weight, key_weight, value_weight, query_weight,
-        out_weight, mlp_up, mlp_down, return_weight, gate_weight, conv,
+        pool_weight, key_weight, value_weight, query_weight, out_weight, mlp_up, mlp_down, return_weight, gate_weight,
+        conv,
     )
     blocks = (cols + 2 * HALF) // 2
     layer_rows = band_tokens + HALF * ((blocks + 7) // 8 * 8)
@@ -508,7 +516,10 @@
     state, context = call(
         functools.partial(second_kernel, cols, bands),
         "context",
-        (place, sums, other_sums, attn_norm_gain[None], mlp_norm_gain[None], *fetched),
+        (
+            place, sums, other_sums, embed, flags, exact, above, below, left, right, attn_norm_gain[None],
+            mlp_norm_gain[None], bit_weight, *fetched,
+        ),
         [array(rows * cols, channels, BF16), array(band_tokens, embed_width, BF16)],
         patch_scratch(rows, cols, channels)
         + [
@@ -521,7 +532,7 @@
             pltpu.VMEM((layer_rows, embed_width), BF16), pltpu.SemaphoreType.DMA((len(fetched) + 2,)),
         ]
         + [pltpu.VMEM(value.shape, value.dtype) for value in fetched],
-        in_hbm=range(5, 5 + len(fetched)),
+        in_hbm=range(13, 13 + len(fetched)),
         scalars=(0,),
         flops=2 * flops,
     )

time: 110 us -> 109 us (level)
  waiting for transfers between devices: 20.8 us -> 19.3 us
    ppermute x1, starting transfers between devices: 2.99 us -> 0.46 us  [local(): other_sums = lax.ppermute(sums, 'core', swap)]
    ppermute x8, waiting for transfers between devices: 18.5 us -> 16.6 us  [shifted(): return lax.ppermute(value, axis, pairs)]
    all_to_all x1, starting transfers between devices: 3.85 us -> 5.02 us  [local(): lax.all_to_all(pieces.reshape(chips, half_tokens, channels), 'chip', 0, 0)]
  transfers between devices with their start and end apart: 13 -> 13, of which waited for: 7 -> 8; matrix products, arithmetic and copies ran while one was open for 1% -> 1% of each run, Pallas kernels for 16% -> 16%
where the time goes in v1:
time: 109 us; the launch traced here: 108 us
  Pallas kernels  47.1 us (43%)
  starting transfers between devices  33.5 us (31%)
  waiting for transfers between devices  19.3 us (18%)
  local copies, waits for them, and re-layouts  6.5 us (6%)
    pallas_call x8, Pallas kernels, call(): pl.pallas_call(kernel, out_shape=outs, in_specs=[spec(index) for index in...  47.1 us
    ppermute x8, starting transfers between devices, shifted(): return lax.ppermute(value, axis, pairs)  17.2 us
    ppermute x8, waiting for transfers between devices, shifted(): return lax.ppermute(value, axis, pairs)  16.6 us
    unnamed x38, local copies, waits for them, and re-layouts  6.5 us
    all_to_all x1, starting transfers between devices, local(): lax.all_to_all(pieces.reshape(chips, half_tokens, channels), 'chip', 0, 0)  5.02 us
    all_to_all x1, starting transfers between devices, local(): lax.all_to_all(sums.reshape(bands, half_tokens, channels), 'ctx', 0, 0)  4.15 us
    all_to_all x1, starting transfers between devices, local(): lax.all_to_all(embed.reshape(bands, band_tokens, -1), 'ctx', 0, 0)  3.53 us
    ppermute x1, starting transfers between devices, local(): received = lax.ppermute(given, 'core', swap)  3.15 us
  transfers between devices with their start and end apart: 13, of which 8 were waited for; matrix products, arithmetic and copies ran while one was open for 1% of the time, Pallas kernels for 16%

profile of v1, /device:TPU:0, one launch (start us, length us, event | category | flops | bytes accessed | tf_op | source)
XLA Modules:
  0.0 108.1 jit_solution(13096626510816919962)
XLA Ops:
  0.6 0.0 copy-start
  0.6 0.9 copy-done
  1.6 0.0 copy-start.6
  1.6 0.8 copy-done.6
  2.4 0.0 copy-start.9
  2.4 0.7 copy-done.9
  3.1 0.3 message.1
  3.4 0.0 copy-start.10
  3.5 0.0 copy-start.11
  3.5 4.9 %collective-permute-start = (bf16[128,640]{1,0:T(8,128)(2,1)S(1)}, bf16[128,640]{1,0:T(8,128)(2,1)S(1)}, u32[]{:S(2)}, u32[]{:S(2)}) collective-permute-start(bf16[128,640]{1,0:T(8,128)(2,1)S(1)} %get-tuple-element.43.bottom), channel_id=1, source_target_pairs={{0,8},{8,16},{16,24},{1,9},{9,17},{17,25},{2,10},{10,18},{18,26},{... | collective-permute-start | bytes 491528 | tf_op jit(solution)/shard_map/ppermute | solution.py:28
  8.3 1.3 %collective-permute-start.1 = (bf16[128,640]{1,0:T(8,128)(2,1)S(1)}, bf16[128,640]{1,0:T(8,128)(2,1)S(1)}, u32[]{:S(2)}, u32[]{:S(2)}) collective-permute-start(bf16[128,640]{1,0:T(8,128)(2,1)S(1)} %get-tuple-element.39.top), channel_id=1, source_target_pairs={{8,0},{16,8},{24,16},{9,1},{17,9},{25,17},{10,2},{18,10},{26,18},{... | collective-permute-start | bytes 491528 | tf_op jit(solution)/shard_map/ppermute | solution.py:28
  9.6 2.2 %prepare.1 = (bf16[128,1024]{1,0:T(8,128)(2,1)}, bf16[512,1024]{1,0:T(8,128)(2,1)}) custom-call(f32[2,512]{1,0:T(2,128)} %candidate_bits.1, f32[2,512]{1,0:T(2,128)} %gate_bits.1, f32[1,512]{1,0:T(1,128)} %bitcast.22, bf16[128,1024]{1,0:T(8,128)(2,1)} %embed), custom_call_target="tpu_custom_call" | custom-call | bytes 8388608 | tf_op jit(solution)/shard_map/prepare/pallas_call | solution.py:83
  11.8 0.7 pad_add_fusion.place
  12.5 0.0 collective-permute-done.above.refs_0_
  12.5 0.0 copy-start.1
  12.5 4.8 %collective-permute-done.1.below.refs_1_ = bf16[128,640]{1,0:T(8,128)(2,1)S(1)} collective-permute-done((bf16[128,640]{1,0:T(8,128)(2,1)S(1)}, bf16[128,640]{1,0:T(8,128)(2,1)S(1)}, u32[]{:S(2)}, u32[]{:S(2)}) %collective-permute-start.1) | collective-permute-done | bytes 163872 | tf_op jit(solution)/shard_map/ppermute | solution.py:28
  17.2 0.0 copy-start.2
  17.3 1.3 %collective-permute-start.2 = (bf16[64,640]{1,0:T(8,128)(2,1)S(1)}, bf16[64,640]{1,0:T(8,128)(2,1)S(1)}, u32[]{:S(2)}, u32[]{:S(2)}) collective-permute-start(bf16[64,640]{1,0:T(8,128)(2,1)S(1)} %get-tuple-element.49), channel_id=1, source_target_pairs={{0,1},{1,2},{2,3},{3,4},{4,5},{5,6},{6,7},{8,9},{9,10},{10,11},{11... | collective-permute-start | bytes 245768 | tf_op jit(solution)/shard_map/ppermute | solution.py:28
  18.6 1.3 %collective-permute-start.3 = (bf16[64,640]{1,0:T(8,128)(2,1)S(1)}, bf16[64,640]{1,0:T(8,128)(2,1)S(1)}, u32[]{:S(2)}, u32[]{:S(2)}) collective-permute-start(bf16[64,640]{1,0:T(8,128)(2,1)S(1)} %get-tuple-element.50), channel_id=1, source_target_pairs={{1,0},{2,1},{3,2},{4,3},{5,4},{6,5},{7,6},{9,8},{10,9},{11,10},{12... | collective-permute-start | bytes 245768 | tf_op jit(solution)/shard_map/ppermute | solution.py:28
  19.9 3.5 %all-to-all-start = ((bf16[4,128,1024]{2,1,0:T(8,128)(2,1)}), bf16[4,128,1024]{2,1,0:T(8,128)(2,1)S(1)}, u32[]{:S(2)}, u32[]{:S(2)}) async-start(bf16[4,128,1024]{2,1,0:T(8,128)(2,1)} %bitcast.19), calls=%async_computation | async-start | bytes 2097152 | tf_op jit(solution)/shard_map/all_to_all | solution.py:457
  23.4 0.0 collective-permute-done.2.refs_2_
  23.4 0.0 copy-start.17
  23.4 0.1 collective-permute-done.3.refs_3_
  23.5 0.0 copy-start.18
  23.5 0.0 copy-done.10
  23.5 0.0 copy-done.11
  23.5 0.0 copy-done.1
  23.5 0.0 copy-done.2
  23.6 0.5 copy-done.17
  24.0 0.1 copy-done.18
  24.2 15.6 %rounds.1 = (f32[256,512]{1,0:T(8,128)}, f32[64,512]{1,0:T(8,128)}, bf16[64,512]{1,0:T(8,128)(2,1)}, bf16[640,128]{1,0:T(8,128)(2,1)}, bf16[128,512]{1,0:T(8,128...) custom-call(s32[2]{0:T(128)} %pad_add_fusion.place, ...), custom_call_target="tpu_custom_call" | custom-call | flops 8053063680 | bytes 1048576 | tf_op jit(solution)/shard_map/rounds/pallas_call | solution.py:83
  39.7 0.0 all-to-all-done
  39.7 0.0 copy-start.12
  39.7 3.2 %collective-permute-start.4 = (bf16[64,512]{1,0:T(8,128)(2,1)}, bf16[64,512]{1,0:T(8,128)(2,1)S(1)}, u32[]{:S(2)}, u32[]{:S(2)}) collective-permute-start(bf16[64,512]{1,0:T(8,128)(2,1)} %get-tuple-element.55), channel_id=1, source_target_pairs={{0,1},{1,0},{2,3},{3,2},{4,5},{5,4},{6,7},{7,6},{8,9},{9,8},{10,11... | collective-permute-start | bytes 196616 | tf_op jit(solution)/shard_map/ppermute | solution.py:482
  42.9 1.1 %collective-permute-done.4.received = bf16[64,512]{1,0:T(8,128)(2,1)S(1)} collective-permute-done((bf16[64,512]{1,0:T(8,128)(2,1)}, bf16[64,512]{1,0:T(8,128)(2,1)S(1)}, u32[]{:S(2)}, u32[]{:S(2)}) %collective-permute-start.4) | collective-permute-done | bytes 65568 | tf_op jit(solution)/shard_map/ppermute | solution.py:482
  44.0 0.9 copy-done.3
  44.9 0.7 pair.1
  45.6 5.0 %all-to-all-start.1 = ((bf16[4,64,512]{2,1,0:T(8,128)(2,1)}), bf16[4,64,512]{2,1,0:T(8,128)(2,1)S(1)}, u32[]{:S(2)}, u32[]{:S(2)}) async-start(bf16[4,64,512]{2,1,0:T(8,128)(2,1)} %bitcast.8), calls=%async_computation.1 | async-start | bytes 524288 | tf_op jit(solution)/shard_map/all_to_all | solution.py:486
  50.7 1.8 %collective-permute-start.5 = (bf16[32,512]{1,0:T(8,128)(2,1)}, bf16[32,512]{1,0:T(8,128)(2,1)S(1)}, u32[]{:S(2)}, u32[]{:S(2)}) collective-permute-start(bf16[32,512]{1,0:T(8,128)(2,1)} %get-tuple-element.58), channel_id=1, source_target_pairs={{0,1},{1,2},{2,3},{3,4},{4,5},{5,6},{6,7},{8,9},{9,10},{10,11},{11... | collective-permute-start | bytes 98312 | tf_op jit(solution)/shard_map/ppermute | solution.py:28
  52.4 1.3 %collective-permute-start.6 = (bf16[32,512]{1,0:T(8,128)(2,1)}, bf16[32,512]{1,0:T(8,128)(2,1)S(1)}, u32[]{:S(2)}, u32[]{:S(2)}) collective-permute-start(bf16[32,512]{1,0:T(8,128)(2,1)} %get-tuple-element.59), channel_id=1, source_target_pairs={{1,0},{2,1},{3,2},{4,3},{5,4},{6,5},{7,6},{9,8},{10,9},{11,10},{12... | collective-permute-start | bytes 98312 | tf_op jit(solution)/shard_map/ppermute | solution.py:28
  53.7 0.0 collective-permute-done.5.left
  53.8 0.0 copy-start.7
  53.8 3.8 %collective-permute-done.6.right = bf16[32,512]{1,0:T(8,128)(2,1)S(1)} collective-permute-done((bf16[32,512]{1,0:T(8,128)(2,1)}, bf16[32,512]{1,0:T(8,128)(2,1)S(1)}, u32[]{:S(2)}, u32[]{:S(2)}) %collective-permute-start.6) | collective-permute-done | bytes 32800 | tf_op jit(solution)/shard_map/ppermute | solution.py:28
  57.5 0.9 copy-done.4
  58.4 0.9 copy-done.5
  59.3 0.1 rows.1
  59.4 0.5 all-to-all-done.1
  59.9 0.7 band.1
  60.6 4.2 %all-to-all-start.2 = ((bf16[4,64,512]{2,1,0:T(8,128)(2,1)}), bf16[4,64,512]{2,1,0:T(8,128)(2,1)S(1)}, u32[]{:S(2)}, u32[]{:S(2)}) async-start(bf16[4,64,512]{2,1,0:T(8,128)(2,1)} %bitcast.10), calls=%async_computation.2 | async-start | bytes 524288 | tf_op jit(solution)/shard_map/all_to_all | solution.py:504
  64.8 3.9 %collective-permute-start.7 = (bf16[160,512]{1,0:T(8,128)(2,1)S(1)}, bf16[160,512]{1,0:T(8,128)(2,1)S(1)}, u32[]{:S(2)}, u32[]{:S(2)}) collective-permute-start(bf16[160,512]{1,0:T(8,128)(2,1)S(1)} %get-tuple-element.66), channel_id=1, source_target_pairs={{0,8},{8,16},{16,24},{1,9},{9,17},{17,25},{2,10},{10,18},{18,26},{... | collective-permute-start | bytes 491528 | tf_op jit(solution)/shard_map/ppermute | solution.py:28
  68.7 1.5 %collective-permute-start.8 = (bf16[160,512]{1,0:T(8,128)(2,1)S(1)}, bf16[160,512]{1,0:T(8,128)(2,1)S(1)}, u32[]{:S(2)}, u32[]{:S(2)}) collective-permute-start(bf16[160,512]{1,0:T(8,128)(2,1)S(1)} %get-tuple-element.67), channel_id=1, source_target_pairs={{8,0},{16,8},{24,16},{9,1},{17,9},{25,17},{10,2},{18,10},{26,18},{... | collective-permute-start | bytes 491528 | tf_op jit(solution)/shard_map/ppermute | solution.py:28
  70.2 2.5 %collective-permute-done.7.above = bf16[160,512]{1,0:T(8,128)(2,1)S(1)} collective-permute-done((bf16[160,512]{1,0:T(8,128)(2,1)S(1)}, bf16[160,512]{1,0:T(8,128)(2,1)S(1)}, u32[]{:S(2)}, u32[]{:S(2)}) %collective-permute-start.7) | collective-permute-done | bytes 163872 | tf_op jit(solution)/shard_map/ppermute | solution.py:28
  72.7 5.4 %collective-permute-done.8.below = bf16[160,512]{1,0:T(8,128)(2,1)S(1)} collective-permute-done((bf16[160,512]{1,0:T(8,128)(2,1)S(1)}, bf16[160,512]{1,0:T(8,128)(2,1)S(1)}, u32[]{:S(2)}, u32[]{:S(2)}) %collective-permute-start.8) | collective-permute-done | bytes 163872 | tf_op jit(solution)/shard_map/ppermute | solution.py:28
  78.1 0.0 all-to-all-done.2
  78.2 0.5 collective-permute-start.9
  78.6 1.2 %collective-permute-done.9.other_sums = bf16[256,512]{1,0:T(8,128)(2,1)S(1)} collective-permute-done((bf16[256,512]{1,0:T(8,128)(2,1)S(1)}, bf16[256,512]{1,0:T(8,128)(2,1)S(1)}, u32[]{:S(2)}, u32[]{:S(2)}) %collective-permute-start.9) | collective-permute-done | bytes 262176 | tf_op jit(solution)/shard_map/ppermute | solution.py:507
  79.8 0.0 copy-done.12
  79.8 0.0 copy-done.7
  79.8 0.0 copy-done.8
  79.8 0.0 copy-done.15
  79.8 0.0 copy-done.16
  79.8 0.0 copy-done.13
  79.8 0.7 copy-done.14
  80.5 27.5 %context.1 = (bf16[256,512]{1,0:T(8,128)(2,1)}, bf16[128,1024]{1,0:T(8,128)(2,1)}) custom-call(s32[2]{0:T(128)} %pad_add_fusion.place, bf16[256,512]{1,0:T(8,128)(2,1)} %bitcast.21, bf16[256,512]{1,0:T(8,128)(2,1)} %copy-done.14, bf16[512,1024]{1,0:T(8,128)(2,1)} %bitcast.18, bf16[640,128]{1,0:T(8,128)(2,1)} %get-tuple-element.70.flags, ...), custom_call_target="tpu_custom_call" | custom-call | flops 16106127360 | bytes 1048576 | tf_op jit(solution)/shard_map/context/pallas_call | solution.py:83
  (9 shorter events, 0.0 us)
Async XLA Ops:
  0.6 1.0 copy-start
  1.6 0.8 copy-start.6
  2.4 0.7 copy-start.9
  3.4 20.1 %copy-start.10 = (bf16[128,640]{1,0:T(8,128)(2,1)}, bf16[128,640]{1,0:T(8,128)(2,1)S(1)}, u32[]{:S(2)}) copy-start(bf16[128,640]{1,0:T(8,128)(2,1)S(1)} %get-tuple-element.39.top) | copy-start | bytes 491524
  3.5 20.1 %copy-start.11 = (bf16[128,640]{1,0:T(8,128)(2,1)}, bf16[128,640]{1,0:T(8,128)(2,1)S(1)}, u32[]{:S(2)}) copy-start(bf16[128,640]{1,0:T(8,128)(2,1)S(1)} %get-tuple-element.43.bottom) | copy-start | bytes 491524
  3.5 9.0 %collective-permute-start = (bf16[128,640]{1,0:T(8,128)(2,1)S(1)}, bf16[128,640]{1,0:T(8,128)(2,1)S(1)}, u32[]{:S(2)}, u32[]{:S(2)}) collective-permute-start(bf16[128,640]{1,0:T(8,128)(2,1)S(1)} %get-tuple-element.43.bottom), channel_id=1, source_target_pairs={{0,8},{8,16},{16,24},{1,9},{9,17},{17,25},{2,10},{10,18},{18,26},{... | collective-permute-start | bytes 491528 | tf_op jit(solution)/shard_map/ppermute | solution.py:28
  8.3 8.9 %collective-permute-start.1 = (bf16[128,640]{1,0:T(8,128)(2,1)S(1)}, bf16[128,640]{1,0:T(8,128)(2,1)S(1)}, u32[]{:S(2)}, u32[]{:S(2)}) collective-permute-start(bf16[128,640]{1,0:T(8,128)(2,1)S(1)} %get-tuple-element.39.top), channel_id=1, source_target_pairs={{8,0},{16,8},{24,16},{9,1},{17,9},{25,17},{10,2},{18,10},{26,18},{... | collective-permute-start | bytes 491528 | tf_op jit(solution)/shard_map/ppermute | solution.py:28
  12.5 11.1 %copy-start.1 = (bf16[128,640]{1,0:T(8,128)(2,1)}, bf16[128,640]{1,0:T(8,128)(2,1)S(1)}, u32[]{:S(2)}) copy-start(bf16[128,640]{1,0:T(8,128)(2,1)S(1)} %collective-permute-done.above.refs_0_) | copy-start | bytes 491524
  17.2 6.3 %copy-start.2 = (bf16[128,640]{1,0:T(8,128)(2,1)}, bf16[128,640]{1,0:T(8,128)(2,1)S(1)}, u32[]{:S(2)}) copy-start(bf16[128,640]{1,0:T(8,128)(2,1)S(1)} %collective-permute-done.1.below.refs_1_) | copy-start | bytes 491524
  17.3 6.1 %collective-permute-start.2 = (bf16[64,640]{1,0:T(8,128)(2,1)S(1)}, bf16[64,640]{1,0:T(8,128)(2,1)S(1)}, u32[]{:S(2)}, u32[]{:S(2)}) collective-permute-start(bf16[64,640]{1,0:T(8,128)(2,1)S(1)} %get-tuple-element.49), channel_id=1, source_target_pairs={{0,1},{1,2},{2,3},{3,4},{4,5},{5,6},{6,7},{8,9},{9,10},{10,11},{11... | collective-permute-start | bytes 245768 | tf_op jit(solution)/shard_map/ppermute | solution.py:28
  18.6 5.0 %collective-permute-start.3 = (bf16[64,640]{1,0:T(8,128)(2,1)S(1)}, bf16[64,640]{1,0:T(8,128)(2,1)S(1)}, u32[]{:S(2)}, u32[]{:S(2)}) collective-permute-start(bf16[64,640]{1,0:T(8,128)(2,1)S(1)} %get-tuple-element.50), channel_id=1, source_target_pairs={{1,0},{2,1},{3,2},{4,3},{5,4},{6,5},{7,6},{9,8},{10,9},{11,10},{12... | collective-permute-start | bytes 245768 | tf_op jit(solution)/shard_map/ppermute | solution.py:28
  19.9 19.9 %all-to-all-start = ((bf16[4,128,1024]{2,1,0:T(8,128)(2,1)}), bf16[4,128,1024]{2,1,0:T(8,128)(2,1)S(1)}, u32[]{:S(2)}, u32[]{:S(2)}) async-start(bf16[4,128,1024]{2,1,0:T(8,128)(2,1)} %bitcast.19), calls=%async_computation | async-start | bytes 2097152 | tf_op jit(solution)/shard_map/all_to_all | solution.py:457
  23.4 0.6 copy-start.17
  23.5 0.6 copy-start.18
  39.7 40.0 %copy-start.12 = (bf16[4,128,1024]{2,1,0:T(8,128)(2,1)}, bf16[4,128,1024]{2,1,0:T(8,128)(2,1)S(1)}, u32[]{:S(2)}) copy-start(bf16[4,128,1024]{2,1,0:T(8,128)(2,1)S(1)} %all-to-all-done) | copy-start | bytes 3145732
  39.7 4.3 %collective-permute-start.4 = (bf16[64,512]{1,0:T(8,128)(2,1)}, bf16[64,512]{1,0:T(8,128)(2,1)S(1)}, u32[]{:S(2)}, u32[]{:S(2)}) collective-permute-start(bf16[64,512]{1,0:T(8,128)(2,1)} %get-tuple-element.55), channel_id=1, source_target_pairs={{0,1},{1,0},{2,3},{3,2},{4,5},{5,4},{6,7},{7,6},{8,9},{9,8},{10,11... | collective-permute-start | bytes 196616 | tf_op jit(solution)/shard_map/ppermute | solution.py:482
  44.0 0.9 copy-start.3
  45.6 14.3 %all-to-all-start.1 = ((bf16[4,64,512]{2,1,0:T(8,128)(2,1)}), bf16[4,64,512]{2,1,0:T(8,128)(2,1)S(1)}, u32[]{:S(2)}, u32[]{:S(2)}) async-start(bf16[4,64,512]{2,1,0:T(8,128)(2,1)} %bitcast.8), calls=%async_computation.1 | async-start | bytes 524288 | tf_op jit(solution)/shard_map/all_to_all | solution.py:486
  50.7 3.1 %collective-permute-start.5 = (bf16[32,512]{1,0:T(8,128)(2,1)}, bf16[32,512]{1,0:T(8,128)(2,1)S(1)}, u32[]{:S(2)}, u32[]{:S(2)}) collective-permute-start(bf16[32,512]{1,0:T(8,128)(2,1)} %get-tuple-element.58), channel_id=1, source_target_pairs={{0,1},{1,2},{2,3},{3,4},{4,5},{5,6},{6,7},{8,9},{9,10},{10,11},{11... | collective-permute-start | bytes 98312 | tf_op jit(solution)/shard_map/ppermute | solution.py:28
  52.4 5.1 %collective-permute-start.6 = (bf16[32,512]{1,0:T(8,128)(2,1)}, bf16[32,512]{1,0:T(8,128)(2,1)S(1)}, u32[]{:S(2)}, u32[]{:S(2)}) collective-permute-start(bf16[32,512]{1,0:T(8,128)(2,1)} %get-tuple-element.59), channel_id=1, source_target_pairs={{1,0},{2,1},{3,2},{4,3},{5,4},{6,5},{7,6},{9,8},{10,9},{11,10},{12... | collective-permute-start | bytes 98312 | tf_op jit(solution)/shard_map/ppermute | solution.py:28
  53.8 26.0 %copy-start.7 = (bf16[32,512]{1,0:T(8,128)(2,1)}, bf16[32,512]{1,0:T(8,128)(2,1)S(1)}, u32[]{:S(2)}) copy-start(bf16[32,512]{1,0:T(8,128)(2,1)S(1)} %collective-permute-done.5.left) | copy-start | bytes 98308
  57.5 22.3 %copy-start.8 = (bf16[32,512]{1,0:T(8,128)(2,1)}, bf16[32,512]{1,0:T(8,128)(2,1)S(1)}, u32[]{:S(2)}) copy-start(bf16[32,512]{1,0:T(8,128)(2,1)S(1)} %collective-permute-done.6.right) | copy-start | bytes 98308
  57.5 0.9 copy-start.4
  58.4 0.9 copy-start.5
  60.6 17.5 %all-to-all-start.2 = ((bf16[4,64,512]{2,1,0:T(8,128)(2,1)}), bf16[4,64,512]{2,1,0:T(8,128)(2,1)S(1)}, u32[]{:S(2)}, u32[]{:S(2)}) async-start(bf16[4,64,512]{2,1,0:T(8,128)(2,1)} %bitcast.10), calls=%async_computation.2 | async-start | bytes 524288 | tf_op jit(solution)/shard_map/all_to_all | solution.py:504
  64.8 7.9 %collective-permute-start.7 = (bf16[160,512]{1,0:T(8,128)(2,1)S(1)}, bf16[160,512]{1,0:T(8,128)(2,1)S(1)}, u32[]{:S(2)}, u32[]{:S(2)}) collective-permute-start(bf16[160,512]{1,0:T(8,128)(2,1)S(1)} %get-tuple-element.66), channel_id=1, source_target_pairs={{0,8},{8,16},{16,24},{1,9},{9,17},{17,25},{2,10},{10,18},{18,26},{... | collective-permute-start | bytes 491528 | tf_op jit(solution)/shard_map/ppermute | solution.py:28
  68.7 9.4 %collective-permute-start.8 = (bf16[160,512]{1,0:T(8,128)(2,1)S(1)}, bf16[160,512]{1,0:T(8,128)(2,1)S(1)}, u32[]{:S(2)}, u32[]{:S(2)}) collective-permute-start(bf16[160,512]{1,0:T(8,128)(2,1)S(1)} %get-tuple-element.67), channel_id=1, source_target_pairs={{8,0},{16,8},{24,16},{9,1},{17,9},{25,17},{10,2},{18,10},{26,18},{... | collective-permute-start | bytes 491528 | tf_op jit(solution)/shard_map/ppermute | solution.py:28
  72.7 7.1 %copy-start.15 = (bf16[160,512]{1,0:T(8,128)(2,1)}, bf16[160,512]{1,0:T(8,128)(2,1)S(1)}, u32[]{:S(2)}) copy-start(bf16[160,512]{1,0:T(8,128)(2,1)S(1)} %collective-permute-done.7.above) | copy-start | bytes 491524
  78.1 1.7 %copy-start.16 = (bf16[160,512]{1,0:T(8,128)(2,1)}, bf16[160,512]{1,0:T(8,128)(2,1)S(1)}, u32[]{:S(2)}) copy-start(bf16[160,512]{1,0:T(8,128)(2,1)S(1)} %collective-permute-done.8.below) | copy-start | bytes 491524
  78.1 1.7 %copy-start.13 = (bf16[4,64,512]{2,1,0:T(8,128)(2,1)}, bf16[4,64,512]{2,1,0:T(8,128)(2,1)S(1)}, u32[]{:S(2)}) copy-start(bf16[4,64,512]{2,1,0:T(8,128)(2,1)S(1)} %all-to-all-done.2) | copy-start | bytes 786436
  78.2 1.6 %collective-permute-start.9 = (bf16[256,512]{1,0:T(8,128)(2,1)S(1)}, bf16[256,512]{1,0:T(8,128)(2,1)S(1)}, u32[]{:S(2)}, u32[]{:S(2)}) collective-permute-start(bf16[256,512]{1,0:T(8,128)(2,1)S(1)} %bitcast.20), channel_id=1, source_target_pairs={{0,1},{1,0},{2,3},{3,2},{4,5},{5,4},{6,7},{7,6},{8,9},{9,8},{10,11... | collective-permute-start | bytes 786440 | tf_op jit(solution)/shard_map/ppermute | solution.py:507
  79.8 0.7 copy-start.14

commit v2 on v1

--- a/solution.py
+++ b/solution.py
@@ -231,7 +231,7 @@
                 flag = self.bits[first : first + size]
                 rounded = self.taps[slot, first : first + size, channels : 2 * channels]
                 candidate = matmul(flag, bit_weight[:, :channels])
-                if step == 0:
+                if step == 0 and waits:
                     third = conv.shape[0] // 3
                     for a in range(3):
                         waits[a].wait()
@@ -337,8 +337,8 @@
     targets = refs[16:]
     pool_weight, key_weight, value_weight, query_weight, out_weight = targets[:5]
     up_weight, down_weight, return_weight, gate_weight, conv = targets[5:]
-    copies = fetch((*sources[:-1], *thirds(sources[-1])), (*targets[:-1], *thirds(conv)), sems)
-    for copy in copies:
+    copies = fetch(sources, targets, sems)
+    for copy in copies[:2]:
         copy.start()
     patch = Patch(cols, state, taps, bits, mask)
     own_half = place[1]
@@ -352,9 +352,13 @@
             part = jnp.where(own_half == half, *pair).astype(BF16)
             sums_all[pl.ds(band * band_tokens + half * half_tokens, half_tokens)] = part
     copies[0].wait()
-    total = embed[...].astype(F32) + matmul(sums_all[...], pool_weight[...])
-    tokens_all[...] = total
-    normed_all[...] = rms_norm(total, attn_gain[...]).astype(BF16)
+    for copy in copies[2:4]:
+        copy.start()
+    for band in range(bands):
+        at = pl.ds(band * band_tokens, band_tokens)
+        total = embed[at].astype(F32) + matmul(sums_all[at], pool_weight[...])
+        tokens_all[at] = total
+        normed_all[at] = rms_norm(total, attn_gain[...]).astype(BF16)
 
     mask[...] = mask_of(flags[...])
     region = matmul(flags[...], one_hot(iota((LANES, LANES), 0) == REGION_LANE))
@@ -380,8 +384,12 @@
         normed[into] = matmul(pick, normed_all[at]).astype(BF16)
 
     copies[1].wait()
+    for copy in copies[4:6]:
+        copy.start()
     keys[...] = matmul(normed_all[...], key_weight[...]).astype(BF16)
     copies[2].wait()
+    for copy in copies[6:8]:
+        copy.start()
     values[...] = matmul(normed_all[...], value_weight[...]).astype(BF16)
     copies[3].wait()
     queries = matmul(normed[...], query_weight[...]).astype(BF16)
@@ -392,6 +400,8 @@
         denominator = jnp.sum(weights, axis=-1, keepdims=True)
         attention[:, at] = (matmul(weights.astype(BF16), values[:, at]) / denominator).astype(BF16)
     copies[4].wait()
+    for copy in copies[8:]:
+        copy.start()
     attended = tokens[...] + matmul(attention[...], out_weight[...])
     tokens[...] = attended
     normed[...] = rms_norm(attended, mlp_gain[...]).astype(BF16)
@@ -418,7 +428,9 @@
                 patch.put(at, patch.get(at) + share)
 
     patch.begin()
-    patch.advance(HALF, flags, conv, gate_weight, bit_weight, (*copies[9:], copies[8]))
+    copies[8].wait()
+    copies[9].wait()
+    patch.advance(HALF, flags, conv, gate_weight, bit_weight, ())
     for r in range(patch.rows - 2 * patch.width):
         state_out[r * cols : (r + 1) * cols] = patch.own(r).astype(BF16)
 
@@ -529,7 +541,7 @@
             pltpu.VMEM((count, LANES), F32),
             pltpu.VMEM((layer_rows, embed_width), F32), pltpu.VMEM((layer_rows, embed_width), BF16),
             pltpu.VMEM((layer_rows, embed_width), BF16), pltpu.VMEM((layer_rows, mlp_up.shape[1]), BF16),
-            pltpu.VMEM((layer_rows, embed_width), BF16), pltpu.SemaphoreType.DMA((len(fetched) + 2,)),
+            pltpu.VMEM((layer_rows, embed_width), BF16), pltpu.SemaphoreType.DMA((len(fetched),)),
         ]
         + [pltpu.VMEM(value.shape, value.dtype) for value in fetched],
         in_hbm=range(13, 13 + len(fetched)),

time: 109 us -> 109 us (level)
  no operation moved by 1% of the time
where the time goes in v2:
time: 109 us; the launch traced here: 108 us
  Pallas kernels  46.8 us (43%)
  starting transfers between devices  33.5 us (31%)
  waiting for transfers between devices  19.3 us (18%)
  local copies, waits for them, and re-layouts  6.5 us (6%)
    pallas_call x8, Pallas kernels, call(): pl.pallas_call(kernel, out_shape=outs, in_specs=[spec(index) for index in...  46.8 us
    ppermute x8, starting transfers between devices, shifted(): return lax.ppermute(value, axis, pairs)  17.2 us
    ppermute x8, waiting for transfers between devices, shifted(): return lax.ppermute(value, axis, pairs)  16.6 us
    unnamed x38, local copies, waits for them, and re-layouts  6.5 us
    all_to_all x1, starting transfers between devices, local(): lax.all_to_all(pieces.reshape(chips, half_tokens, channels), 'chip', 0, 0)  5.02 us
    all_to_all x1, starting transfers between devices, local(): lax.all_to_all(sums.reshape(bands, half_tokens, channels), 'ctx', 0, 0)  4.15 us
    all_to_all x1, starting transfers between devices, local(): lax.all_to_all(embed.reshape(bands, band_tokens, -1), 'ctx', 0, 0)  3.53 us
    ppermute x1, starting transfers between devices, local(): received = lax.ppermute(given, 'core', swap)  3.15 us
  transfers between devices with their start and end apart: 13, of which 8 were waited for; matrix products, arithmetic and copies ran while one was open for 1% of the time, Pallas kernels for 16%

profile of v2, /device:TPU:0, one launch (start us, length us, event | category | flops | bytes accessed | tf_op | source)
XLA Modules:
  0.0 107.9 jit_solution(3908210067184704902)
XLA Ops:
  0.6 0.0 copy-start
  0.6 0.9 copy-done
  1.6 0.8 copy-done.6
  2.4 0.7 copy-done.9
  3.1 0.3 message.1
  3.4 0.0 copy-start.10
  3.5 0.0 copy-start.11
  3.5 4.9 %collective-permute-start = (bf16[128,640]{1,0:T(8,128)(2,1)S(1)}, bf16[128,640]{1,0:T(8,128)(2,1)S(1)}, u32[]{:S(2)}, u32[]{:S(2)}) collective-permute-start(bf16[128,640]{1,0:T(8,128)(2,1)S(1)} %get-tuple-element.43.bottom), channel_id=1, source_target_pairs={{0,8},{8,16},{16,24},{1,9},{9,17},{17,25},{2,10},{10,18},{18,26},{... | collective-permute-start | bytes 491528 | tf_op jit(solution)/shard_map/ppermute | solution.py:28
  8.3 1.3 %collective-permute-start.1 = (bf16[128,640]{1,0:T(8,128)(2,1)S(1)}, bf16[128,640]{1,0:T(8,128)(2,1)S(1)}, u32[]{:S(2)}, u32[]{:S(2)}) collective-permute-start(bf16[128,640]{1,0:T(8,128)(2,1)S(1)} %get-tuple-element.39.top), channel_id=1, source_target_pairs={{8,0},{16,8},{24,16},{9,1},{17,9},{25,17},{10,2},{18,10},{26,18},{... | collective-permute-start | bytes 491528 | tf_op jit(solution)/shard_map/ppermute | solution.py:28
  9.6 2.2 %prepare.1 = (bf16[128,1024]{1,0:T(8,128)(2,1)}, bf16[512,1024]{1,0:T(8,128)(2,1)}) custom-call(f32[2,512]{1,0:T(2,128)} %candidate_bits.1, f32[2,512]{1,0:T(2,128)} %gate_bits.1, f32[1,512]{1,0:T(1,128)} %bitcast.22, bf16[128,1024]{1,0:T(8,128)(2,1)} %embed), custom_call_target="tpu_custom_call" | custom-call | bytes 8388608 | tf_op jit(solution)/shard_map/prepare/pallas_call | solution.py:83
  11.8 0.7 pad_add_fusion.place
  12.5 0.0 collective-permute-done.above.refs_0_
  12.5 0.0 copy-start.1
  12.5 4.8 %collective-permute-done.1.below.refs_1_ = bf16[128,640]{1,0:T(8,128)(2,1)S(1)} collective-permute-done((bf16[128,640]{1,0:T(8,128)(2,1)S(1)}, bf16[128,640]{1,0:T(8,128)(2,1)S(1)}, u32[]{:S(2)}, u32[]{:S(2)}) %collective-permute-start.1) | collective-permute-done | bytes 163872 | tf_op jit(solution)/shard_map/ppermute | solution.py:28
  17.2 0.0 copy-start.2
  17.3 1.3 %collective-permute-start.2 = (bf16[64,640]{1,0:T(8,128)(2,1)S(1)}, bf16[64,640]{1,0:T(8,128)(2,1)S(1)}, u32[]{:S(2)}, u32[]{:S(2)}) collective-permute-start(bf16[64,640]{1,0:T(8,128)(2,1)S(1)} %get-tuple-element.49), channel_id=1, source_target_pairs={{0,1},{1,2},{2,3},{3,4},{4,5},{5,6},{6,7},{8,9},{9,10},{10,11},{11... | collective-permute-start | bytes 245768 | tf_op jit(solution)/shard_map/ppermute | solution.py:28
  18.6 1.3 %collective-permute-start.3 = (bf16[64,640]{1,0:T(8,128)(2,1)S(1)}, bf16[64,640]{1,0:T(8,128)(2,1)S(1)}, u32[]{:S(2)}, u32[]{:S(2)}) collective-permute-start(bf16[64,640]{1,0:T(8,128)(2,1)S(1)} %get-tuple-element.50), channel_id=1, source_target_pairs={{1,0},{2,1},{3,2},{4,3},{5,4},{6,5},{7,6},{9,8},{10,9},{11,10},{12... | collective-permute-start | bytes 245768 | tf_op jit(solution)/shard_map/ppermute | solution.py:28
  19.9 3.5 %all-to-all-start = ((bf16[4,128,1024]{2,1,0:T(8,128)(2,1)}), bf16[4,128,1024]{2,1,0:T(8,128)(2,1)S(1)}, u32[]{:S(2)}, u32[]{:S(2)}) async-start(bf16[4,128,1024]{2,1,0:T(8,128)(2,1)} %bitcast.19), calls=%async_computation | async-start | bytes 2097152 | tf_op jit(solution)/shard_map/all_to_all | solution.py:469
  23.4 0.0 collective-permute-done.2.refs_2_
  23.4 0.0 copy-start.17
  23.4 0.1 collective-permute-done.3.refs_3_
  23.5 0.0 copy-start.18
  23.5 0.0 copy-done.10
  23.5 0.0 copy-done.11
  23.5 0.0 copy-done.1
  23.5 0.0 copy-done.2
  23.6 0.5 copy-done.17
  24.0 0.1 copy-done.18
  24.2 15.6 %rounds.1 = (f32[256,512]{1,0:T(8,128)}, f32[64,512]{1,0:T(8,128)}, bf16[64,512]{1,0:T(8,128)(2,1)}, bf16[640,128]{1,0:T(8,128)(2,1)}, bf16[128,512]{1,0:T(8,128...) custom-call(s32[2]{0:T(128)} %pad_add_fusion.place, ...), custom_call_target="tpu_custom_call" | custom-call | flops 8053063680 | bytes 1048576 | tf_op jit(solution)/shard_map/rounds/pallas_call | solution.py:83
  39.7 0.0 all-to-all-done
  39.7 0.0 copy-start.12
  39.7 3.2 %collective-permute-start.4 = (bf16[64,512]{1,0:T(8,128)(2,1)}, bf16[64,512]{1,0:T(8,128)(2,1)S(1)}, u32[]{:S(2)}, u32[]{:S(2)}) collective-permute-start(bf16[64,512]{1,0:T(8,128)(2,1)} %get-tuple-element.55), channel_id=1, source_target_pairs={{0,1},{1,0},{2,3},{3,2},{4,5},{5,4},{6,7},{7,6},{8,9},{9,8},{10,11... | collective-permute-start | bytes 196616 | tf_op jit(solution)/shard_map/ppermute | solution.py:494
  42.9 1.1 %collective-permute-done.4.received = bf16[64,512]{1,0:T(8,128)(2,1)S(1)} collective-permute-done((bf16[64,512]{1,0:T(8,128)(2,1)}, bf16[64,512]{1,0:T(8,128)(2,1)S(1)}, u32[]{:S(2)}, u32[]{:S(2)}) %collective-permute-start.4) | collective-permute-done | bytes 65568 | tf_op jit(solution)/shard_map/ppermute | solution.py:494
  44.0 0.0 copy-start.3
  44.0 0.9 copy-done.3
  44.9 0.7 pair.1
  45.6 5.0 %all-to-all-start.1 = ((bf16[4,64,512]{2,1,0:T(8,128)(2,1)}), bf16[4,64,512]{2,1,0:T(8,128)(2,1)S(1)}, u32[]{:S(2)}, u32[]{:S(2)}) async-start(bf16[4,64,512]{2,1,0:T(8,128)(2,1)} %bitcast.8), calls=%async_computation.1 | async-start | bytes 524288 | tf_op jit(solution)/shard_map/all_to_all | solution.py:498
  50.7 1.8 %collective-permute-start.5 = (bf16[32,512]{1,0:T(8,128)(2,1)}, bf16[32,512]{1,0:T(8,128)(2,1)S(1)}, u32[]{:S(2)}, u32[]{:S(2)}) collective-permute-start(bf16[32,512]{1,0:T(8,128)(2,1)} %get-tuple-element.58), channel_id=1, source_target_pairs={{0,1},{1,2},{2,3},{3,4},{4,5},{5,6},{6,7},{8,9},{9,10},{10,11},{11... | collective-permute-start | bytes 98312 | tf_op jit(solution)/shard_map/ppermute | solution.py:28
  52.4 1.3 %collective-permute-start.6 = (bf16[32,512]{1,0:T(8,128)(2,1)}, bf16[32,512]{1,0:T(8,128)(2,1)S(1)}, u32[]{:S(2)}, u32[]{:S(2)}) collective-permute-start(bf16[32,512]{1,0:T(8,128)(2,1)} %get-tuple-element.59), channel_id=1, source_target_pairs={{1,0},{2,1},{3,2},{4,3},{5,4},{6,5},{7,6},{9,8},{10,9},{11,10},{12... | collective-permute-start | bytes 98312 | tf_op jit(solution)/shard_map/ppermute | solution.py:28
  53.7 0.0 collective-permute-done.5.left
  53.8 0.0 copy-start.7
  53.8 3.8 %collective-permute-done.6.right = bf16[32,512]{1,0:T(8,128)(2,1)S(1)} collective-permute-done((bf16[32,512]{1,0:T(8,128)(2,1)}, bf16[32,512]{1,0:T(8,128)(2,1)S(1)}, u32[]{:S(2)}, u32[]{:S(2)}) %collective-permute-start.6) | collective-permute-done | bytes 32800 | tf_op jit(solution)/shard_map/ppermute | solution.py:28
  57.5 0.0 copy-start.8
  57.5 0.9 copy-done.4
  58.4 0.9 copy-done.5
  59.3 0.1 rows.1
  59.4 0.5 all-to-all-done.1
  59.9 0.7 band.1
  60.6 4.2 %all-to-all-start.2 = ((bf16[4,64,512]{2,1,0:T(8,128)(2,1)}), bf16[4,64,512]{2,1,0:T(8,128)(2,1)S(1)}, u32[]{:S(2)}, u32[]{:S(2)}) async-start(bf16[4,64,512]{2,1,0:T(8,128)(2,1)} %bitcast.10), calls=%async_computation.2 | async-start | bytes 524288 | tf_op jit(solution)/shard_map/all_to_all | solution.py:516
  64.8 3.9 %collective-permute-start.7 = (bf16[160,512]{1,0:T(8,128)(2,1)S(1)}, bf16[160,512]{1,0:T(8,128)(2,1)S(1)}, u32[]{:S(2)}, u32[]{:S(2)}) collective-permute-start(bf16[160,512]{1,0:T(8,128)(2,1)S(1)} %get-tuple-element.66), channel_id=1, source_target_pairs={{0,8},{8,16},{16,24},{1,9},{9,17},{17,25},{2,10},{10,18},{18,26},{... | collective-permute-start | bytes 491528 | tf_op jit(solution)/shard_map/ppermute | solution.py:28
  68.7 1.5 %collective-permute-start.8 = (bf16[160,512]{1,0:T(8,128)(2,1)S(1)}, bf16[160,512]{1,0:T(8,128)(2,1)S(1)}, u32[]{:S(2)}, u32[]{:S(2)}) collective-permute-start(bf16[160,512]{1,0:T(8,128)(2,1)S(1)} %get-tuple-element.67), channel_id=1, source_target_pairs={{8,0},{16,8},{24,16},{9,1},{17,9},{25,17},{10,2},{18,10},{26,18},{... | collective-permute-start | bytes 491528 | tf_op jit(solution)/shard_map/ppermute | solution.py:28
  70.2 2.5 %collective-permute-done.7.above = bf16[160,512]{1,0:T(8,128)(2,1)S(1)} collective-permute-done((bf16[160,512]{1,0:T(8,128)(2,1)S(1)}, bf16[160,512]{1,0:T(8,128)(2,1)S(1)}, u32[]{:S(2)}, u32[]{:S(2)}) %collective-permute-start.7) | collective-permute-done | bytes 163872 | tf_op jit(solution)/shard_map/ppermute | solution.py:28
  72.7 5.4 %collective-permute-done.8.below = bf16[160,512]{1,0:T(8,128)(2,1)S(1)} collective-permute-done((bf16[160,512]{1,0:T(8,128)(2,1)S(1)}, bf16[160,512]{1,0:T(8,128)(2,1)S(1)}, u32[]{:S(2)}, u32[]{:S(2)}) %collective-permute-start.8) | collective-permute-done | bytes 163872 | tf_op jit(solution)/shard_map/ppermute | solution.py:28
  78.1 0.0 all-to-all-done.2
  78.2 0.5 collective-permute-start.9
  78.6 1.2 %collective-permute-done.9.other_sums = bf16[256,512]{1,0:T(8,128)(2,1)S(1)} collective-permute-done((bf16[256,512]{1,0:T(8,128)(2,1)S(1)}, bf16[256,512]{1,0:T(8,128)(2,1)S(1)}, u32[]{:S(2)}, u32[]{:S(2)}) %collective-permute-start.9) | collective-permute-done | bytes 262176 | tf_op jit(solution)/shard_map/ppermute | solution.py:519
  79.8 0.0 copy-done.12
  79.8 0.0 copy-done.7
  79.8 0.0 copy-done.8
  79.8 0.0 copy-done.15
  79.8 0.0 copy-done.16
  79.8 0.0 copy-done.13
  79.8 0.7 copy-done.14
  80.5 27.2 %context.1 = (bf16[256,512]{1,0:T(8,128)(2,1)}, bf16[128,1024]{1,0:T(8,128)(2,1)}) custom-call(s32[2]{0:T(128)} %pad_add_fusion.place, bf16[256,512]{1,0:T(8,128)(2,1)} %bitcast.21, bf16[256,512]{1,0:T(8,128)(2,1)} %copy-done.14, bf16[512,1024]{1,0:T(8,128)(2,1)} %bitcast.18, bf16[640,128]{1,0:T(8,128)(2,1)} %get-tuple-element.70.flags, ...), custom_call_target="tpu_custom_call" | custom-call | flops 16106127360 | bytes 1048576 | tf_op jit(solution)/shard_map/context/pallas_call | solution.py:83
  (9 shorter events, 0.0 us)
Async XLA Ops:
  0.6 1.0 copy-start
  1.6 0.8 copy-start.6
  2.4 0.7 copy-start.9
  3.4 20.1 %copy-start.10 = (bf16[128,640]{1,0:T(8,128)(2,1)}, bf16[128,640]{1,0:T(8,128)(2,1)S(1)}, u32[]{:S(2)}) copy-start(bf16[128,640]{1,0:T(8,128)(2,1)S(1)} %get-tuple-element.39.top) | copy-start | bytes 491524
  3.5 20.1 %copy-start.11 = (bf16[128,640]{1,0:T(8,128)(2,1)}, bf16[128,640]{1,0:T(8,128)(2,1)S(1)}, u32[]{:S(2)}) copy-start(bf16[128,640]{1,0:T(8,128)(2,1)S(1)} %get-tuple-element.43.bottom) | copy-start | bytes 491524
  3.5 9.0 %collective-permute-start = (bf16[128,640]{1,0:T(8,128)(2,1)S(1)}, bf16[128,640]{1,0:T(8,128)(2,1)S(1)}, u32[]{:S(2)}, u32[]{:S(2)}) collective-permute-start(bf16[128,640]{1,0:T(8,128)(2,1)S(1)} %get-tuple-element.43.bottom), channel_id=1, source_target_pairs={{0,8},{8,16},{16,24},{1,9},{9,17},{17,25},{2,10},{10,18},{18,26},{... | collective-permute-start | bytes 491528 | tf_op jit(solution)/shard_map/ppermute | solution.py:28
  8.3 8.9 %collective-permute-start.1 = (bf16[128,640]{1,0:T(8,128)(2,1)S(1)}, bf16[128,640]{1,0:T(8,128)(2,1)S(1)}, u32[]{:S(2)}, u32[]{:S(2)}) collective-permute-start(bf16[128,640]{1,0:T(8,128)(2,1)S(1)} %get-tuple-element.39.top), channel_id=1, source_target_pairs={{8,0},{16,8},{24,16},{9,1},{17,9},{25,17},{10,2},{18,10},{26,18},{... | collective-permute-start | bytes 491528 | tf_op jit(solution)/shard_map/ppermute | solution.py:28
  12.5 11.1 %copy-start.1 = (bf16[128,640]{1,0:T(8,128)(2,1)}, bf16[128,640]{1,0:T(8,128)(2,1)S(1)}, u32[]{:S(2)}) copy-start(bf16[128,640]{1,0:T(8,128)(2,1)S(1)} %collective-permute-done.above.refs_0_) | copy-start | bytes 491524
  17.2 6.3 %copy-start.2 = (bf16[128,640]{1,0:T(8,128)(2,1)}, bf16[128,640]{1,0:T(8,128)(2,1)S(1)}, u32[]{:S(2)}) copy-start(bf16[128,640]{1,0:T(8,128)(2,1)S(1)} %collective-permute-done.1.below.refs_1_) | copy-start | bytes 491524
  17.3 6.1 %collective-permute-start.2 = (bf16[64,640]{1,0:T(8,128)(2,1)S(1)}, bf16[64,640]{1,0:T(8,128)(2,1)S(1)}, u32[]{:S(2)}, u32[]{:S(2)}) collective-permute-start(bf16[64,640]{1,0:T(8,128)(2,1)S(1)} %get-tuple-element.49), channel_id=1, source_target_pairs={{0,1},{1,2},{2,3},{3,4},{4,5},{5,6},{6,7},{8,9},{9,10},{10,11},{11... | collective-permute-start | bytes 245768 | tf_op jit(solution)/shard_map/ppermute | solution.py:28
  18.6 5.0 %collective-permute-start.3 = (bf16[64,640]{1,0:T(8,128)(2,1)S(1)}, bf16[64,640]{1,0:T(8,128)(2,1)S(1)}, u32[]{:S(2)}, u32[]{:S(2)}) collective-permute-start(bf16[64,640]{1,0:T(8,128)(2,1)S(1)} %get-tuple-element.50), channel_id=1, source_target_pairs={{1,0},{2,1},{3,2},{4,3},{5,4},{6,5},{7,6},{9,8},{10,9},{11,10},{12... | collective-permute-start | bytes 245768 | tf_op jit(solution)/shard_map/ppermute | solution.py:28
  19.9 19.9 %all-to-all-start = ((bf16[4,128,1024]{2,1,0:T(8,128)(2,1)}), bf16[4,128,1024]{2,1,0:T(8,128)(2,1)S(1)}, u32[]{:S(2)}, u32[]{:S(2)}) async-start(bf16[4,128,1024]{2,1,0:T(8,128)(2,1)} %bitcast.19), calls=%async_computation | async-start | bytes 2097152 | tf_op jit(solution)/shard_map/all_to_all | solution.py:469
  23.4 0.6 copy-start.17
  23.5 0.6 copy-start.18
  39.7 40.0 %copy-start.12 = (bf16[4,128,1024]{2,1,0:T(8,128)(2,1)}, bf16[4,128,1024]{2,1,0:T(8,128)(2,1)S(1)}, u32[]{:S(2)}) copy-start(bf16[4,128,1024]{2,1,0:T(8,128)(2,1)S(1)} %all-to-all-done) | copy-start | bytes 3145732
  39.7 4.3 %collective-permute-start.4 = (bf16[64,512]{1,0:T(8,128)(2,1)}, bf16[64,512]{1,0:T(8,128)(2,1)S(1)}, u32[]{:S(2)}, u32[]{:S(2)}) collective-permute-start(bf16[64,512]{1,0:T(8,128)(2,1)} %get-tuple-element.55), channel_id=1, source_target_pairs={{0,1},{1,0},{2,3},{3,2},{4,5},{5,4},{6,7},{7,6},{8,9},{9,8},{10,11... | collective-permute-start | bytes 196616 | tf_op jit(solution)/shard_map/ppermute | solution.py:494
  44.0 0.9 copy-start.3
  45.6 14.3 %all-to-all-start.1 = ((bf16[4,64,512]{2,1,0:T(8,128)(2,1)}), bf16[4,64,512]{2,1,0:T(8,128)(2,1)S(1)}, u32[]{:S(2)}, u32[]{:S(2)}) async-start(bf16[4,64,512]{2,1,0:T(8,128)(2,1)} %bitcast.8), calls=%async_computation.1 | async-start | bytes 524288 | tf_op jit(solution)/shard_map/all_to_all | solution.py:498
  50.7 3.1 %collective-permute-start.5 = (bf16[32,512]{1,0:T(8,128)(2,1)}, bf16[32,512]{1,0:T(8,128)(2,1)S(1)}, u32[]{:S(2)}, u32[]{:S(2)}) collective-permute-start(bf16[32,512]{1,0:T(8,128)(2,1)} %get-tuple-element.58), channel_id=1, source_target_pairs={{0,1},{1,2},{2,3},{3,4},{4,5},{5,6},{6,7},{8,9},{9,10},{10,11},{11... | collective-permute-start | bytes 98312 | tf_op jit(solution)/shard_map/ppermute | solution.py:28
  52.4 5.1 %collective-permute-start.6 = (bf16[32,512]{1,0:T(8,128)(2,1)}, bf16[32,512]{1,0:T(8,128)(2,1)S(1)}, u32[]{:S(2)}, u32[]{:S(2)}) collective-permute-start(bf16[32,512]{1,0:T(8,128)(2,1)} %get-tuple-element.59), channel_id=1, source_target_pairs={{1,0},{2,1},{3,2},{4,3},{5,4},{6,5},{7,6},{9,8},{10,9},{11,10},{12... | collective-permute-start | bytes 98312 | tf_op jit(solution)/shard_map/ppermute | solution.py:28
  53.8 26.0 %copy-start.7 = (bf16[32,512]{1,0:T(8,128)(2,1)}, bf16[32,512]{1,0:T(8,128)(2,1)S(1)}, u32[]{:S(2)}) copy-start(bf16[32,512]{1,0:T(8,128)(2,1)S(1)} %collective-permute-done.5.left) | copy-start | bytes 98308
  57.5 22.3 %copy-start.8 = (bf16[32,512]{1,0:T(8,128)(2,1)}, bf16[32,512]{1,0:T(8,128)(2,1)S(1)}, u32[]{:S(2)}) copy-start(bf16[32,512]{1,0:T(8,128)(2,1)S(1)} %collective-permute-done.6.right) | copy-start | bytes 98308
  57.5 0.9 copy-start.4
  58.4 0.9 copy-start.5
  60.6 17.5 %all-to-all-start.2 = ((bf16[4,64,512]{2,1,0:T(8,128)(2,1)}), bf16[4,64,512]{2,1,0:T(8,128)(2,1)S(1)}, u32[]{:S(2)}, u32[]{:S(2)}) async-start(bf16[4,64,512]{2,1,0:T(8,128)(2,1)} %bitcast.10), calls=%async_computation.2 | async-start | bytes 524288 | tf_op jit(solution)/shard_map/all_to_all | solution.py:516
  64.8 7.9 %collective-permute-start.7 = (bf16[160,512]{1,0:T(8,128)(2,1)S(1)}, bf16[160,512]{1,0:T(8,128)(2,1)S(1)}, u32[]{:S(2)}, u32[]{:S(2)}) collective-permute-start(bf16[160,512]{1,0:T(8,128)(2,1)S(1)} %get-tuple-element.66), channel_id=1, source_target_pairs={{0,8},{8,16},{16,24},{1,9},{9,17},{17,25},{2,10},{10,18},{18,26},{... | collective-permute-start | bytes 491528 | tf_op jit(solution)/shard_map/ppermute | solution.py:28
  68.7 9.4 %collective-permute-start.8 = (bf16[160,512]{1,0:T(8,128)(2,1)S(1)}, bf16[160,512]{1,0:T(8,128)(2,1)S(1)}, u32[]{:S(2)}, u32[]{:S(2)}) collective-permute-start(bf16[160,512]{1,0:T(8,128)(2,1)S(1)} %get-tuple-element.67), channel_id=1, source_target_pairs={{8,0},{16,8},{24,16},{9,1},{17,9},{25,17},{10,2},{18,10},{26,18},{... | collective-permute-start | bytes 491528 | tf_op jit(solution)/shard_map/ppermute | solution.py:28
  72.7 7.1 %copy-start.15 = (bf16[160,512]{1,0:T(8,128)(2,1)}, bf16[160,512]{1,0:T(8,128)(2,1)S(1)}, u32[]{:S(2)}) copy-start(bf16[160,512]{1,0:T(8,128)(2,1)S(1)} %collective-permute-done.7.above) | copy-start | bytes 491524
  78.1 1.7 %copy-start.16 = (bf16[160,512]{1,0:T(8,128)(2,1)}, bf16[160,512]{1,0:T(8,128)(2,1)S(1)}, u32[]{:S(2)}) copy-start(bf16[160,512]{1,0:T(8,128)(2,1)S(1)} %collective-permute-done.8.below) | copy-start | bytes 491524
  78.1 1.7 %copy-start.13 = (bf16[4,64,512]{2,1,0:T(8,128)(2,1)}, bf16[4,64,512]{2,1,0:T(8,128)(2,1)S(1)}, u32[]{:S(2)}) copy-start(bf16[4,64,512]{2,1,0:T(8,128)(2,1)S(1)} %all-to-all-done.2) | copy-start | bytes 786436
  78.2 1.6 %collective-permute-start.9 = (bf16[256,512]{1,0:T(8,128)(2,1)S(1)}, bf16[256,512]{1,0:T(8,128)(2,1)S(1)}, u32[]{:S(2)}, u32[]{:S(2)}) collective-permute-start(bf16[256,512]{1,0:T(8,128)(2,1)S(1)} %bitcast.20), channel_id=1, source_target_pairs={{0,1},{1,0},{2,3},{3,2},{4,5},{5,4},{6,7},{7,6},{8,9},{9,8},{10,11... | collective-permute-start | bytes 786440 | tf_op jit(solution)/shard_map/ppermute | solution.py:519
  79.8 0.7 copy-start.14
